TPU v7x, 32 devices: a whole 2x2x4 slice. The times are simulated.
32 devices in a mesh: req: 8 (over z, y), mp: 4 (over x, core).
Axes of the slice: x: 2, y: 2, z: 4, core: 2. Of those that a mesh axis runs over, the one named last changes fastest.
Arguments:
- hidden_in: bfloat16 [8192, 2048], P('req', 'mp'), may hold values from -6 to 6
- w_qkv: bfloat16 [3, 2048, 2048], P(None, 'req', 'mp'), may hold values from -0.125 to 0.125
- w_out: bfloat16 [2048, 2048], P('mp', 'req'), may hold values from -0.125 to 0.125
- attn_gain: bfloat16 [2048], replicated, may hold values from 0.099609375 to 1.8984375
- mlp_gain: bfloat16 [2048], replicated, may hold values from 0.099609375 to 1.8984375
- w_gate: bfloat16 [2048, 8192], P('req', 'mp'), may hold values from -0.125 to 0.125
- w_up: bfloat16 [2048, 8192], P('req', 'mp'), may hold values from -0.125 to 0.125
- w_down: bfloat16 [8192, 2048], P('mp', 'req'), may hold values from -0.0625 to 0.0625
- k_cache: bfloat16 [8, 4096, 2048], P('req', None, 'mp'), may hold values from -363 to 363
- v_cache: bfloat16 [8, 4096, 2048], P('req', None, 'mp'), may hold values from -6 to 6
- cache_len: int32 [8], P('req'), may hold values from 256 to 4096, as said below
Outputs:
- hidden_out: bfloat16 [8192, 2048], P('req', 'mp')
- new_keys: bfloat16 [8192, 2048], P('req', 'mp')
- new_values: bfloat16 [8192, 2048], P('req', 'mp')
Inputs may be any that keep to these rules, and one draw needn't show every extreme that they name: Each request uses its first cache_len slots; later slots hold unused data. Some request's cache is full in every draw.
All inputs are finite; a program needn't handle non-finite values.
Results may differ from a plain program's by a relative error of at most 0.02.
Values may be sent and summed in bfloat16 or wider, within the bound.
A program may use at most 128 MiB of HBM per device.

v0:
```python
import jax
import jax.numpy as jnp
from jax import lax
from jax.sharding import PartitionSpec as P

HD = 64


THETA = 130000.0
EPSILON = 1e-05
NEG_FILL = -1e30


def rms_scale(rows, gain):
    values = rows.astype(jnp.float32)
    meansq = jnp.mean(values * values, axis=-1, keepdims=True)
    return (values * lax.rsqrt(meansq + EPSILON) * gain.astype(jnp.float32)).astype(jnp.bfloat16)


def rotate(tensor, positions):
    half = tensor.shape[-1] // 2
    freq = THETA ** (-(jnp.arange(half, dtype=jnp.float32) * 2.0 / tensor.shape[-1]))
    angle = positions[:, None, None] * freq[None, None, :]
    cosine = jnp.cos(angle)
    sine = jnp.sin(angle)
    first = tensor[..., :half]
    second = tensor[..., half:]
    return jnp.concatenate(
        [first * cosine - second * sine, second * cosine + first * sine], axis=-1
    )


def absorb(carry, queries, keys, values, valid):
    top, total, accum = carry
    scores = jnp.einsum("qhd,khd->hqk", queries, keys, preferred_element_type=jnp.float32) * HD ** (
        -0.5
    )
    scores = jnp.where(valid[None], scores, NEG_FILL)
    new_top = jnp.maximum(top, jnp.max(scores, axis=-1, keepdims=True))
    factor = jnp.exp(top - new_top)
    probs = jnp.where(valid[None], jnp.exp(scores - new_top), 0.0)
    total = total * factor + jnp.sum(probs, axis=-1, keepdims=True)
    accum = accum * factor + jnp.einsum(
        "hqk,khd->hqd", probs.astype(jnp.bfloat16), values, preferred_element_type=jnp.float32
    )
    return (new_top, total, accum)


def on_device(
    hidden_in, w_qkv, w_out, attn_gain, mlp_gain, w_gate, w_up, w_down, k_cache, v_cache, cache_len
):
    new_count = hidden_in.shape[0]
    width = w_qkv.shape[2]
    heads_local = width // HD
    slots = k_cache.shape[1]
    full_rows = lax.all_gather(hidden_in, "mp", axis=1, tiled=True)
    normed = rms_scale(full_rows, attn_gain)
    columns = normed
    projected = jnp.einsum(
        "nd,kdw->knw",
        columns,
        lax.all_gather(w_qkv, "req", axis=1, tiled=True),
        preferred_element_type=jnp.float32,
    )
    length = cache_len[0]
    positions = (length + jnp.arange(new_count, dtype=jnp.int32)).astype(jnp.float32)
    queries = rotate(projected[0].reshape(new_count, heads_local, HD), positions).astype(
        jnp.bfloat16
    )
    fresh_keys = rotate(projected[1].reshape(new_count, heads_local, HD), positions).astype(
        jnp.bfloat16
    )
    fresh_values = projected[2].astype(jnp.bfloat16).reshape(new_count, heads_local, HD)
    rows = jnp.arange(new_count, dtype=jnp.int32)
    causal = rows[:, None] >= rows[None, :]
    start_carry = (
        jnp.full((heads_local, new_count, 1), NEG_FILL, jnp.float32),
        jnp.zeros((heads_local, new_count, 1), jnp.float32),
        jnp.zeros((heads_local, new_count, HD), jnp.float32),
    )
    carry = absorb(start_carry, queries, fresh_keys, fresh_values, causal)
    cache_keys = k_cache[0].reshape(slots, heads_local, HD)
    cache_values = v_cache[0].reshape(slots, heads_local, HD)
    block = min(slots, 512)
    count = (length + block - 1) // block

    def step_block(index, state):
        begin = index * block
        keys = lax.dynamic_slice_in_dim(cache_keys, begin, block, 0)
        values = lax.dynamic_slice_in_dim(cache_values, begin, block, 0)
        valid = (begin + jnp.arange(block, dtype=jnp.int32) < length)[None, :]
        return absorb(state, queries, keys, values, valid)

    top, total, accum = lax.fori_loop(0, count, step_block, carry)
    attn = (accum / total).transpose(1, 0, 2).reshape(new_count, width).astype(jnp.bfloat16)
    partial_value = jnp.dot(
        attn, lax.all_gather(w_out, "req", axis=1, tiled=True), preferred_element_type=jnp.float32
    )
    summed = lax.psum_scatter(
        partial_value.astype(jnp.bfloat16), "mp", scatter_dimension=1, tiled=True
    ).astype(jnp.float32)
    mid_local = (hidden_in.astype(jnp.float32) + summed).astype(jnp.bfloat16)
    mid_full = lax.all_gather(mid_local, "mp", axis=1, tiled=True)
    normed2 = rms_scale(mid_full, mlp_gain)
    columns = normed2
    gate = jnp.dot(
        columns,
        lax.all_gather(w_gate, "req", axis=0, tiled=True),
        preferred_element_type=jnp.float32,
    )
    upper = jnp.dot(
        columns, lax.all_gather(w_up, "req", axis=0, tiled=True), preferred_element_type=jnp.float32
    )
    units = (jax.nn.silu(gate) * upper).astype(jnp.bfloat16)
    terms = jnp.dot(
        units, lax.all_gather(w_down, "req", axis=1, tiled=True), preferred_element_type=jnp.float32
    )
    reduced = lax.psum_scatter(
        terms.astype(jnp.bfloat16), "mp", scatter_dimension=1, tiled=True
    ).astype(jnp.float32)
    hidden_out = (mid_local.astype(jnp.float32) + reduced).astype(jnp.bfloat16)
    return (
        hidden_out,
        fresh_keys.reshape(new_count, width),
        fresh_values.reshape(new_count, width),
    )


def solution(mesh):
    return jax.shard_map(
        on_device,
        mesh=mesh,
        in_specs=(
            P("req", "mp"),
            P(None, "req", "mp"),
            P("mp", "req"),
            P(),
            P(),
            P("req", "mp"),
            P("req", "mp"),
            P("mp", "req"),
            P("req", None, "mp"),
            P("req", None, "mp"),
            P("req"),
        ),
        out_specs=(P("req", "mp"), P("req", "mp"), P("req", "mp")),
        check_vma=False,
    )
```

profile of v0, /device:TPU:0, one launch (start us, length us, event | category | flops | bytes accessed | tf_op | source)
XLA Modules:
  0.0 873.9 jit_solution(479641056278675463)
XLA Ops:
  12.7 6.5 copy.17
  19.2 6.6 copy.18
  26.3 20.4 %all-gather.8.cloned.1.call-done = bf16[1024,2048]{1,0:T(8,128)(2,1)} async-done(((bf16[1024,512]{1,0:T(8,128)(2,1)}), bf16[1024,2048]{1,0:T(8,128)(2,1)}) %all-gather.8.cloned.1.call-update) | async-done | bytes 4194320 | tf_op jit(solution)/shard_map/all_gather | solution.py:56
  49.9 99.5 %all-gather.10.cloned.1.call-done = bf16[3,2048,512]{1,2,0:T(8,128)(2,1)} async-done(((bf16[3,256,512]{1,2,0:T(8,128)(2,1)}), bf16[3,2048,512]{1,2,0:T(8,128)(2,1)}) %all-gather.10.cloned.1.call-update) | async-done | bytes 6291472 | tf_op jit(solution)/shard_map/all_gather | solution.py:62
  149.4 10.2 %fusion.39 = f32[3,1024,512]{1,2,0:T(8,128)S(1)} fusion(bf16[3,2048,512]{1,2,0:T(8,128)(2,1)} %all-gather.10.cloned.1.call-done, bf16[1024,2048]{1,0:T(8,128)(2,1)} %all-gather.8.cloned.1.call-done, f32[2048]{0:T(1024)S(1)} %convert_element_type.87, f32[1024]{0:T(1024)S(1)} %add_rsqrt_fusion.1), kind=kOutput, calls=%fused_computation.51 | convolution fusion | flops 6450839552 | bytes 16789504 | tf_op jit(solution)/shard_map/nd,kdw->knw/dot_general | solution.py:59
  162.4 13.6 %fusion.19 = (f32[8,1024]{1,0:T(8,128)S(1)}, f32[8,1024,1024]{1,2,0:T(8,128)}) fusion(pred[1024,1024]{0,1:T(8,128)(4,1)S(1)} %iota_compare_fusion, bf16[1024,8,32]{0,2,1:T(8,128)(2,1)S(1)} %get-tuple-element.82, bf16[1024,8,32]{0,2,1:T(8,128)(2,1)S(1)} %get-tuple-element.81, bf16[1024,8,32]{0,2,1:T(8,128)(2,1)S(1)} %get-tuple-element.84, ...), kind=kOutput, calls=%fused_computation.26 | convolution fusion | flops 1103093760 | bytes 36732928 | tf_op jit(solution)/shard_map/qhd,khd->hqk/dot_general | solution.py:35
  176.0 14.9 %fusion.21 = f32[8,1024]{1,0:T(8,128)S(1)} fusion(f32[8,1024,1024]{1,2,0:T(8,128)} %get-tuple-element.91, f32[8,1024]{1,0:T(8,128)S(1)} %get-tuple-element.87, pred[1024,1024]{0,1:T(8,128)(4,1)S(1)} %iota_compare_fusion), kind=kLoop, calls=%fused_computation.28 | loop fusion | flops 41934848 | bytes 34668544 | tf_op jit(solution)/shard_map/reduce_sum | solution.py:42
  191.0 16.9 %fusion.42 = f32[8,1024,64]{1,2,0:T(8,128)} fusion(bf16[1024,8,64]{0,2,1:T(8,128)(2,1)S(1)} %bitcast.80, f32[8,1024,1024]{1,2,0:T(8,128)} %get-tuple-element.91, f32[8,1024]{1,0:T(8,128)S(1)} %get-tuple-element.87, pred[1024,1024]{0,1:T(8,128)(4,1)S(1)} %iota_compare_fusion, f32[8,1024]{1,0:T(8,128)S(1)} %get-tuple-element.85), kind=kOutput, calls=%fused_computation.57 | convolution fusion | flops 1116209152 | bytes 37814272 | tf_op jit(solution)/shard_map/hqk,khd->hqd/dot_general | solution.py:43
  207.8 30.0 %while.14 = (s32[]{:T(128)}, f32[8,1024,1]{1,0,2:T(8,128)S(1)}, f32[8,1024,1]{1,0,2:T(8,128)S(1)}, f32[8,1024,64]{1,2,0:T(8,128)}, s32[]{:T(128)}, /*index=5*/s3...) while((s32[]{:T(128)}, f32[8,1024,1]{1,0,2:T(8,128)S(1)}, ...), condition=%wide.region_6.7_spmd, body=%wide.region_3.6_spmd.sunk | while | flops 1129341952 | bytes 73927416 | solution.py:94
  208.5 4.4 bitcast_reduce_fusion.2
  212.9 5.2 multiply_add_fusion.3
  218.1 4.7 fusion.73
  228.0 5.2 multiply_add_fusion.3
  233.2 4.7 fusion.73
  239.8 6.0 convolution_convert_fusion
  245.9 132.9 %reduce-scatter.3.cloned.1.call-done = bf16[1024,512]{1,0:T(8,128)(2,1)} async-done(((bf16[1024,2048]{1,0:T(8,128)(2,1)}), bf16[1024,512]{1,0:T(8,128)(2,1)}) %reduce-scatter.3.cloned.1.call-update) | async-done | bytes 1048592 | tf_op jit(solution)/shard_map/reduce_scatter | solution.py:99
  383.4 8.5 reduce-scatter.5.cloned.1.call-start
  391.9 24.0 %all-gather.14.cloned.1.call-done = bf16[1024,2048]{1,0:T(8,128)(2,1)} async-done(((bf16[1024,512]{1,0:T(8,128)(2,1)}), bf16[1024,2048]{1,0:T(8,128)(2,1)}) %all-gather.14.cloned.1.call-update) | async-done | bytes 4194320 | tf_op jit(solution)/shard_map/all_gather | solution.py:103
  419.0 124.1 %all-gather.16.cloned.1.call-done = bf16[2048,2048]{1,0:T(8,128)(2,1)} async-done(((bf16[256,2048]{1,0:T(8,128)(2,1)}), bf16[2048,2048]{1,0:T(8,128)(2,1)}) %all-gather.16.cloned.1.call-update) | async-done | bytes 8388624 | tf_op jit(solution)/shard_map/all_gather | solution.py:108
  543.1 14.7 %fusion.47 = f32[1024,2048]{1,0:T(8,128)} fusion(bf16[2048,2048]{1,0:T(8,128)(2,1)} %all-gather.16.cloned.1.call-done, bf16[1024,2048]{1,0:T(8,128)(2,1)} %all-gather.14.cloned.1.call-done, f32[2048]{0:T(1024)S(1)} %convert_element_type.102, f32[1024]{0:T(1024)S(1)} %add_rsqrt_fusion), kind=kOutput, calls=%fused_computation.58 | convolution fusion | flops 8598323200 | bytes 20983808 | tf_op jit(solution)/shard_map/dot_general | solution.py:106
  557.8 110.8 %all-gather.18.cloned.1.call-done = bf16[2048,2048]{1,0:T(8,128)(2,1)} async-done(((bf16[256,2048]{1,0:T(8,128)(2,1)}), bf16[2048,2048]{1,0:T(8,128)(2,1)}) %all-gather.18.cloned.1.call-update) | async-done | bytes 8388624 | tf_op jit(solution)/shard_map/all_gather | solution.py:112
  668.6 125.8 %all-gather.20.cloned.1.call-done = bf16[2048,2048]{1,0:T(8,128)(2,1)} async-done(((bf16[2048,256]{1,0:T(8,128)(2,1)}), bf16[2048,2048]{1,0:T(8,128)(2,1)}) %all-gather.20.cloned.1.call-update) | async-done | bytes 8388624 | tf_op jit(solution)/shard_map/all_gather | solution.py:116
  794.5 27.3 %fusion.38 = bf16[1024,2048]{1,0:T(8,128)(2,1)} fusion(bf16[2048,2048]{1,0:T(8,128)(2,1)} %all-gather.20.cloned.1.call-done, f32[1024,2048]{1,0:T(8,128)} %fusion.47, bf16[2048,2048]{1,0:T(8,128)(2,1)} %all-gather.18.cloned.1.call-done, bf16[1024,2048]{1,0:T(8,128)(2,1)} %all-gather.14.cloned.1.call-done, f32[2048]{0:T(1024)S(1)} %convert_element_type.102, ...), kind=kOutput, calls=%fused_computation.50 | convolution fusion | flops 17202937856 | bytes 33566720 | tf_op jit(solution)/shard_map/dot_general | solution.py:115
  826.3 38.4 %reduce-scatter.5.cloned.1.call-done = bf16[1024,512]{1,0:T(8,128)(2,1)} async-done(((bf16[1024,2048]{1,0:T(8,128)(2,1)}), bf16[1024,512]{1,0:T(8,128)(2,1)}) %reduce-scatter.5.cloned.1.call-update) | async-done | bytes 1048592 | tf_op jit(solution)/shard_map/reduce_scatter | solution.py:118
  (76 shorter events, 33.5 us)
Async XLA Ops:
  7.2 39.6 %all-gather.8.cloned.1.call-start = ((), (), s32[]{:S(2)}) async-start(), calls=%async_computation.2 | async-start | bytes 5242880 | tf_op jit(solution)/shard_map/all_gather | solution.py:56
  7.9 141.5 %all-gather.10.cloned.1.call-start = ((), (), s32[]{:S(2)}) async-start(), calls=%async_computation.3 | async-start | bytes 7077888 | tf_op jit(solution)/shard_map/all_gather | solution.py:62
  10.3 229.5 %all-gather.12.cloned.1.call-start = ((), (), s32[]{:S(2)}) async-start(), calls=%async_computation.4 | async-start | bytes 2359296 | tf_op jit(solution)/shard_map/all_gather | solution.py:97
  11.0 367.8 %reduce-scatter.3.cloned.1.call-start = ((), (), s32[]{:S(2)}) async-start(), calls=%async_computation.5 | async-start | bytes 5242880 | tf_op jit(solution)/shard_map/reduce_scatter | solution.py:99
  159.6 2.6 copy-start.1
  162.2 13.8 %copy-start.5 = (bf16[1024,8,32]{0,2,1:T(8,128)(2,1)}, bf16[1024,8,32]{0,2,1:T(8,128)(2,1)S(1)}, u32[]{:S(2)}) copy-start(bf16[1024,8,32]{0,2,1:T(8,128)(2,1)S(1)} %get-tuple-element.83) | copy-start | bytes 1572868
  162.2 13.8 %copy-start.7 = (bf16[1024,8,32]{0,2,1:T(8,128)(2,1)}, bf16[1024,8,32]{0,2,1:T(8,128)(2,1)S(1)}, u32[]{:S(2)}) copy-start(bf16[1024,8,32]{0,2,1:T(8,128)(2,1)S(1)} %get-tuple-element.84) | copy-start | bytes 1572868
  208.5 4.4 copy-start.3
  218.1 4.7 copy-start.4
  223.5 4.4 copy-start.3
  233.2 4.7 copy-start.4
  239.8 139.0 %copy-start.2 = (bf16[1024,512]{1,0:T(8,128)(2,1)S(1)}, bf16[1024,512]{1,0:T(8,128)(2,1)}, u32[]{:S(2)}) copy-start(bf16[1024,512]{1,0:T(8,128)(2,1)} %param.13) | copy-start | bytes 3145732
  245.8 146.1 %copy-start.9 = (bf16[2048]{0:T(1024)(128)(2,1)S(1)}, bf16[2048]{0:T(1024)(128)(2,1)}, u32[]{:S(2)}) copy-start(bf16[2048]{0:T(1024)(128)(2,1)} %param.17) | copy-start | bytes 12292
  245.8 170.1 %all-gather.14.cloned.1.call-start = ((), (), s32[]{:S(2)}) async-start(), calls=%async_computation.6 | async-start | bytes 5242880 | tf_op jit(solution)/shard_map/all_gather | solution.py:103
  381.3 161.8 %all-gather.16.cloned.1.call-start = ((), (), s32[]{:S(2)}) async-start(), calls=%async_computation.7 | async-start | bytes 9437184 | tf_op jit(solution)/shard_map/all_gather | solution.py:108
  381.9 286.7 %all-gather.18.cloned.1.call-start = ((), (), s32[]{:S(2)}) async-start(), calls=%async_computation.8 | async-start | bytes 9437184 | tf_op jit(solution)/shard_map/all_gather | solution.py:112
  382.6 411.8 %all-gather.20.cloned.1.call-start = ((), (), s32[]{:S(2)}) async-start(), calls=%async_computation.9 | async-start | bytes 9437184 | tf_op jit(solution)/shard_map/all_gather | solution.py:116
  383.4 481.3 %reduce-scatter.5.cloned.1.call-start = ((), (), s32[]{:S(2)}) async-start(), calls=%async_computation.10 | async-start | bytes 5242880 | tf_op jit(solution)/shard_map/reduce_scatter | solution.py:118
  557.8 264.0 %copy-start.6 = (bf16[1024,8,32]{0,2,1:T(8,128)(2,1)S(1)}, bf16[1024,8,32]{0,2,1:T(8,128)(2,1)}, u32[]{:S(2)}) copy-start(bf16[1024,8,32]{0,2,1:T(8,128)(2,1)} %copy-done.5) | copy-start | bytes 1572868
  557.8 264.0 %copy-start.8 = (bf16[1024,8,32]{0,2,1:T(8,128)(2,1)S(1)}, bf16[1024,8,32]{0,2,1:T(8,128)(2,1)}, u32[]{:S(2)}) copy-start(bf16[1024,8,32]{0,2,1:T(8,128)(2,1)} %copy-done.7) | copy-start | bytes 1572868
  821.8 42.9 %copy-start = (bf16[1024,512]{1,0:T(8,128)(2,1)S(1)}, bf16[1024,512]{1,0:T(8,128)(2,1)}, u32[]{:S(2)}) copy-start(bf16[1024,512]{1,0:T(8,128)(2,1)} %add_convert_fusion.1) | copy-start | bytes 3145732
Sparse Core Ops, SparseCore 0:
  9.6 37.1 all-gather.7
  49.4 99.9 all-gather.9
  151.4 49.2 all-gather.11
  245.9 132.8 reduce-scatter.2
  381.4 34.4 all-gather.13
  418.1 124.9 all-gather.15
  545.5 123.1 all-gather.17
  670.8 123.5 all-gather.19
  821.9 42.6 reduce-scatter.4
where the time goes:
time: 888 us; the launch traced here: 874 us
  waiting for transfers between devices  679 us (76%)
  matrix products  108 us (12%)
  other arithmetic  41 us (5%)
  local copies, waits for them, and re-layouts  21.7 us (2%)
  between operations  14.9 us (2%)
    reduce_scatter x1, waiting for transfers between devices, on_device(): lax.psum_scatter(partial_value.astype(jnp.bfloat16), 'mp', scatter_dimens...  133 us
    all_gather x1, waiting for transfers between devices, on_device(): lax.all_gather(w_down, 'req', axis=1, tiled=True)  126 us
    all_gather x1, waiting for transfers between devices, on_device(): lax.all_gather(w_gate, 'req', axis=0, tiled=True)  124 us
    all_gather x1, waiting for transfers between devices, on_device(): lax.all_gather(w_up, 'req', axis=0, tiled=True)  111 us
    all_gather x1, waiting for transfers between devices, on_device(): lax.all_gather(w_qkv, 'req', axis=1, tiled=True)  99.5 us
    reduce_scatter x1, waiting for transfers between devices, on_device(): lax.psum_scatter(terms.astype(jnp.bfloat16), 'mp', scatter_dimension=1, t...  38.4 us
    dot_general x1, matrix products, on_device(): jnp.dot(units, lax.all_gather(w_down, 'req', axis=1, tiled=True), preferr...  27.3 us
    dot_general x3, matrix products, absorb(): jnp.einsum('hqk,khd->hqd', probs.astype(jnp.bfloat16), values, preferred_...  27.2 us
  transfers between devices with their start and end apart: 9, of which 8 were waited for; matrix products, arithmetic and copies ran while one was open for 15% of the time, Pallas kernels for 0%

commit v1 on v0

v1 whole, which is shorter than its diff:
```python
import functools

import jax
import jax.numpy as jnp
from jax import lax
from jax.experimental import pallas as pl
from jax.experimental.pallas import tpu as pltpu
from jax.sharding import PartitionSpec as P

HD = 64
MESH = pl.DeviceIdType.MESH
LOG2E = 1.4426950408889634
PAIR = 2 * HD

THETA = 130000.0
EPSILON = 1e-05
NEG_FILL = -1e30


def rms_scale(rows, gain):
    values = rows.astype(jnp.float32)
    meansq = jnp.mean(values * values, axis=-1, keepdims=True)
    return (values * lax.rsqrt(meansq + EPSILON) * gain.astype(jnp.float32)).astype(jnp.bfloat16)


def rotate(tensor, positions):
    half = tensor.shape[-1] // 2
    freq = THETA ** (-(jnp.arange(half, dtype=jnp.float32) * 2.0 / tensor.shape[-1]))
    angle = positions[:, None, None] * freq[None, None, :]
    cosine = jnp.cos(angle)
    sine = jnp.sin(angle)
    first = tensor[..., :half]
    second = tensor[..., half:]
    return jnp.concatenate(
        [first * cosine - second * sine, second * cosine + first * sine], axis=-1
    )


def columns_of(ref, index, width):
    return ref.at[:, pl.ds(pl.multiple_of(index * width, width), width)]


class ReqGather:
    def __init__(self, n, pieces, sems):
        self.half = n // 2
        self.pieces = pieces
        self.send_far, self.recv_far, self.send_near, self.recv_near, self.own_sem = sems
        me = lax.axis_index("req")
        self.group, self.parity = me // 2, lax.rem(me, 2)
        self.me, self.partner = me, me + 1 - 2 * self.parity

    def member(self, shift):
        return lax.rem(self.group + shift + self.half, self.half) * 2 + self.parity

    def greet(self, barrier):
        for shift in range(1, self.half):
            pl.semaphore_signal(barrier, inc=1, device_id={"req": self.member(shift)}, device_id_type=MESH)
        pl.semaphore_signal(barrier, inc=1, device_id={"req": self.partner}, device_id_type=MESH)
        return self.half

    def far(self, c, shift):
        src, slot = self.pieces[c]
        return pltpu.make_async_remote_copy(
            src_ref=src, dst_ref=slot(self.me), send_sem=self.send_far.at[c, shift],
            recv_sem=self.recv_far.at[c, shift], device_id={"req": self.member(shift)}, device_id_type=MESH)

    def near(self, c, shift):
        src, slot = self.pieces[c]
        owner = self.member(-shift)
        return pltpu.make_async_remote_copy(
            src_ref=src if shift == 0 else slot(owner), dst_ref=slot(owner), send_sem=self.send_near.at[c, shift],
            recv_sem=self.recv_near.at[c, shift], device_id={"req": self.partner}, device_id_type=MESH)

    def own(self, c):
        src, slot = self.pieces[c]
        return pltpu.make_async_copy(src, slot(self.me), self.own_sem.at[c])

    def start(self, c):
        for shift in range(1, self.half):
            self.far(c, shift).start()
        self.near(c, 0).start()
        self.own(c).start()

    def forward(self, c):
        for shift in range(1, self.half):
            self.far(c, shift).wait_recv()
            self.near(c, shift).start()

    def finish(self, c):
        for shift in range(1, self.half):
            self.far(c, shift).wait_send()
        for shift in range(self.half):
            self.near(c, shift).wait()
        self.own(c).wait()


def gather_sems(pieces, n):
    dma = pltpu.SemaphoreType.DMA
    return [dma((pieces, n // 2)) for _ in range(4)] + [dma((pieces,))]


def first_kernel(n, n_mp, hid, wqkv, hid_full, wqkv_full, *sems):
    mp_send, mp_recv, mp_own = sems[5:]
    depth, width = wqkv.shape[1], hid.shape[1]
    pieces = [
        (wqkv.at[i], lambda r, i=i: wqkv_full.at[i, pl.ds(pl.multiple_of(r * depth, depth), depth)])
        for i in range(3)
    ]
    gather = ReqGather(n, pieces, sems[:5])
    me = lax.axis_index("mp")
    barrier = pltpu.get_barrier_semaphore()
    expected = gather.greet(barrier)
    for shift in range(1, n_mp):
        pl.semaphore_signal(barrier, inc=1, device_id={"mp": lax.rem(me + shift, n_mp)}, device_id_type=MESH)
    pl.semaphore_wait(barrier, expected + n_mp - 1)
    mine = columns_of(hid_full, me, width)
    copies = [
        pltpu.make_async_remote_copy(
            src_ref=hid, dst_ref=mine, send_sem=mp_send.at[shift], recv_sem=mp_recv.at[shift],
            device_id={"mp": lax.rem(me + shift, n_mp)}, device_id_type=MESH)
        for shift in range(1, n_mp)
    ]
    own = pltpu.make_async_copy(hid, mine, mp_own)
    for c in range(3):
        gather.start(c)
    for copy in copies:
        copy.start()
    own.start()
    for c in range(3):
        gather.forward(c)
    for c in range(3):
        gather.finish(c)
    for copy in copies:
        copy.wait()
    own.wait()


def gather_first(n, n_mp, hidden_in, w_qkv):
    rows, width = hidden_in.shape
    dma = pltpu.SemaphoreType.DMA
    hbm = pl.BlockSpec(memory_space=pl.ANY)
    return pl.pallas_call(
        functools.partial(first_kernel, n, n_mp),
        out_shape=(
            jax.ShapeDtypeStruct((rows, width * n_mp), hidden_in.dtype),
            jax.ShapeDtypeStruct((3, w_qkv.shape[1] * n, w_qkv.shape[2]), w_qkv.dtype),
        ),
        in_specs=[hbm, hbm],
        out_specs=(hbm, hbm),
        scratch_shapes=gather_sems(3, n) + [dma((n_mp,)), dma((n_mp,)), dma],
        compiler_params=pltpu.CompilerParams(collective_id=0, has_side_effects=True),
    )(hidden_in, w_qkv)


def attend(length, q_begin, q_ref, kn_ref, vn_ref, kc_ref, vc_ref, out_ref):
    rows = q_ref.shape[0]
    fresh = kn_ref.shape[0]
    slots = kc_ref.shape[1]
    block = min(slots, 512)
    lane = lax.broadcasted_iota(jnp.int32, (1, PAIR), 1)
    masks = (lane < HD, lane >= HD)
    query = q_ref[...]
    queries = [jnp.where(mask, query, 0) for mask in masks]
    row_index = q_begin + lax.broadcasted_iota(jnp.int32, (rows, 1), 0)

    def absorb(state, keys, values, hide):
        out = []
        for mask, mine, (top, accum) in zip(masks, queries, state):
            scores = lax.dot_general(
                mine, keys, (((1,), (1,)), ((), ())), preferred_element_type=jnp.float32)
            scores = hide(scores * (LOG2E * HD**-0.5))
            new_top = jnp.maximum(top, jnp.max(scores, axis=1, keepdims=True))
            probs = jnp.exp2(scores - new_top).astype(jnp.bfloat16)
            extended = jnp.where(mask, values, 1)
            accum = accum * jnp.exp2(top - new_top) + jnp.dot(
                probs, extended, preferred_element_type=jnp.float32)
            out.append((new_top, accum))
        return tuple(out)

    state = tuple(
        (jnp.full((rows, 1), NEG_FILL, jnp.float32), jnp.zeros((rows, PAIR), jnp.float32)) for _ in masks)

    def fresh_step(index, state):
        begin = pl.multiple_of(index * block, block)
        column = begin + lax.broadcasted_iota(jnp.int32, (1, block), 1)
        return absorb(
            state, kn_ref[pl.ds(begin, block)], vn_ref[pl.ds(begin, block)],
            lambda scores: jnp.where(row_index >= column, scores, NEG_FILL))

    def cache_step(index, state):
        begin = pl.multiple_of(index * block, block)
        column = begin + lax.broadcasted_iota(jnp.int32, (1, block), 1)
        bias = jnp.where(column < length, 0.0, NEG_FILL)
        return absorb(
            state, kc_ref[0, pl.ds(begin, block)], vc_ref[0, pl.ds(begin, block)],
            lambda scores: scores + bias)

    state = lax.fori_loop(0, fresh // block, fresh_step, state)
    state = lax.fori_loop(0, slots // block, cache_step, state)
    parts = [accum / pltpu.roll(accum, HD, 1) for _, accum in state]
    out_ref[...] = jnp.where(masks[0], parts[0], parts[1]).astype(out_ref.dtype)


def attention_kernel(
    n, n_pairs, n_blocks, length_ref, q_ref, kn_ref, vn_ref, kc_ref, vc_ref, w_out, w_gate, w_up, w_down,
    out_ref, w_out_full, w_gate_full, w_up_full, w_down_full, *sems
):
    step = pl.program_id(0) * n_blocks + pl.program_id(1)
    steps = n_pairs * n_blocks
    pieces = [(w_out, lambda r: columns_of(w_out_full, r, w_out.shape[1]))]
    for src, full in ((w_gate, w_gate_full), (w_up, w_up_full)):
        depth = src.shape[0]
        for part in range(2):
            rows = depth // 2
            pieces.append((
                src.at[pl.ds(part * rows, rows)],
                lambda r, full=full, part=part, depth=depth, rows=rows: full.at[
                    pl.ds(pl.multiple_of(r * depth + part * rows, rows), rows)]))
    for part in range(2):
        rows, width = w_down.shape[0] // 2, w_down.shape[1]
        pieces.append((
            w_down.at[pl.ds(part * rows, rows)],
            lambda r, part=part, rows=rows, width=width: w_down_full.at[
                pl.ds(part * rows, rows), pl.ds(pl.multiple_of(r * width, width), width)]))
    gather = ReqGather(n, pieces, sems)
    count = len(pieces)

    @pl.when(step == 0)
    def _():
        barrier = pltpu.get_barrier_semaphore()
        pl.semaphore_wait(barrier, gather.greet(barrier))
        for c in range(3):
            gather.start(c)

    attend(
        length_ref[0], pl.program_id(1) * q_ref.shape[0], q_ref, kn_ref, vn_ref, kc_ref, vc_ref, out_ref)

    for c in range(count):
        @pl.when(step == min(c, steps - 1))
        def _(c=c):
            gather.forward(c)
            if c + 3 < count:
                gather.start(c + 3)

    @pl.when(step == steps - 1)
    def _():
        for c in range(count):
            gather.finish(c)


def attend_and_gather(n, length, queries, keys, values, k_cache, v_cache, w_out, w_gate, w_up, w_down):
    rows, width = queries.shape
    slots = k_cache.shape[1]
    n_pairs, n_blocks = width // PAIR, 2
    hbm = pl.BlockSpec(memory_space=pl.ANY)
    row_block = pl.BlockSpec((rows // n_blocks, PAIR), lambda h, i: (i, h))
    whole = pl.BlockSpec((rows, PAIR), lambda h, i: (0, h))
    cached = pl.BlockSpec((1, slots, PAIR), lambda h, i: (0, 0, h))
    like = jax.ShapeDtypeStruct
    return pl.pallas_call(
        functools.partial(attention_kernel, n, n_pairs, n_blocks),
        grid=(n_pairs, n_blocks),
        out_shape=(
            like((rows, width), queries.dtype),
            like((w_out.shape[0], w_out.shape[1] * n), w_out.dtype),
            like((w_gate.shape[0] * n, w_gate.shape[1]), w_gate.dtype),
            like((w_up.shape[0] * n, w_up.shape[1]), w_up.dtype),
            like((w_down.shape[0], w_down.shape[1] * n), w_down.dtype),
        ),
        in_specs=[pl.BlockSpec(memory_space=pltpu.SMEM), row_block, whole, whole, cached, cached] + [hbm] * 4,
        out_specs=(row_block,) + (hbm,) * 4,
        scratch_shapes=gather_sems(7, n),
        compiler_params=pltpu.CompilerParams(
            collective_id=1, has_side_effects=True, vmem_limit_bytes=48 * 1024 * 1024,
            dimension_semantics=("arbitrary", "arbitrary")),
    )(length, queries, keys, values, k_cache, v_cache, w_out, w_gate, w_up, w_down)


def on_device(
    n, n_mp, hidden_in, w_qkv, w_out, attn_gain, mlp_gain, w_gate, w_up, w_down, k_cache, v_cache, cache_len
):
    new_count = hidden_in.shape[0]
    width = w_qkv.shape[2]
    heads_local = width // HD
    full_rows, w_qkv_full = gather_first(n, n_mp, hidden_in, w_qkv)
    normed = rms_scale(full_rows, attn_gain)
    columns = normed
    projected = jnp.einsum(
        "nd,kdw->knw",
        columns,
        w_qkv_full,
        preferred_element_type=jnp.float32,
    )
    length = cache_len[0]
    positions = (length + jnp.arange(new_count, dtype=jnp.int32)).astype(jnp.float32)
    queries = rotate(projected[0].reshape(new_count, heads_local, HD), positions).astype(
        jnp.bfloat16
    )
    fresh_keys = rotate(projected[1].reshape(new_count, heads_local, HD), positions).astype(
        jnp.bfloat16
    )
    fresh_values = projected[2].astype(jnp.bfloat16).reshape(new_count, heads_local, HD)
    attn, w_out_full, w_gate_full, w_up_full, w_down_full = attend_and_gather(
        n, cache_len, queries.reshape(new_count, width), fresh_keys.reshape(new_count, width),
        fresh_values.reshape(new_count, width), k_cache, v_cache, w_out, w_gate, w_up, w_down)
    partial_value = jnp.dot(
        attn, w_out_full, preferred_element_type=jnp.float32
    )
    summed = lax.psum_scatter(
        partial_value.astype(jnp.bfloat16), "mp", scatter_dimension=1, tiled=True
    ).astype(jnp.float32)
    mid_local = (hidden_in.astype(jnp.float32) + summed).astype(jnp.bfloat16)
    mid_full = lax.all_gather(mid_local, "mp", axis=1, tiled=True)
    normed2 = rms_scale(mid_full, mlp_gain)
    columns = normed2
    gate = jnp.dot(
        columns,
        w_gate_full,
        preferred_element_type=jnp.float32,
    )
    upper = jnp.dot(
        columns, w_up_full, preferred_element_type=jnp.float32
    )
    units = (jax.nn.silu(gate) * upper).astype(jnp.bfloat16)
    terms = jnp.dot(
        units, w_down_full, preferred_element_type=jnp.float32
    )
    reduced = lax.psum_scatter(
        terms.astype(jnp.bfloat16), "mp", scatter_dimension=1, tiled=True
    ).astype(jnp.float32)
    hidden_out = (mid_local.astype(jnp.float32) + reduced).astype(jnp.bfloat16)
    return (
        hidden_out,
        fresh_keys.reshape(new_count, width),
        fresh_values.reshape(new_count, width),
    )


def solution(mesh):
    return jax.shard_map(
        functools.partial(on_device, mesh.shape["req"], mesh.shape["mp"]),
        mesh=mesh,
        in_specs=(
            P("req", "mp"),
            P(None, "req", "mp"),
            P("mp", "req"),
            P(),
            P(),
            P("req", "mp"),
            P("req", "mp"),
            P("mp", "req"),
            P("req", None, "mp"),
            P("req", None, "mp"),
            P("req"),
        ),
        out_specs=(P("req", "mp"), P("req", "mp"), P("req", "mp")),
        check_vma=False,
    )
```

time: 888 us -> 664 us (0.75); the launches traced: 874 us -> 664 us
  waiting for transfers between devices: 679 us -> 140 us
  Pallas kernels: 0 us -> 423 us
  matrix products: 108 us -> 58.5 us
  other arithmetic: 41 us -> 15.8 us
  local copies, waits for them, and re-layouts: 21.7 us -> 10.7 us
    all_gather x6 -> x0, waiting for transfers between devices: 481 us -> none  [the longest x1 126 us: on_device(): lax.all_gather(w_down, 'req', axis=1, tiled=True)]
    pallas_call x0 -> x2, Pallas kernels: none -> 423 us  [the longest x1 335 us: attend_and_gather(): pl.pallas_call(functools.partial(attention_kernel, n, n_pairs, n_blocks),...]
    reduce_scatter x1, waiting for transfers between devices: 133 us -> 61.2 us  [on_device(): lax.psum_scatter(partial_value.astype(jnp.bfloat16), 'mp', scatter_dimens...]
    dot_general x10 -> x4, matrix products: 108 us -> 58.5 us  [the longest x1 27.4 us: on_device(): terms = jnp.dot(units, w_down_full, preferred_element_type=jnp.float32)]
    reduce_sum x3 -> x0, other arithmetic: 24.2 us -> none  [absorb(): total = total * factor + jnp.sum(probs, axis=-1, keepdims=True)]
    unnamed x21 -> x14, local copies, waits for them, and re-layouts: 19.5 us -> 1.25 us
    all_gather x1, waiting for transfers between devices: 24 us -> 34.4 us  [on_device(): mid_full = lax.all_gather(mid_local, 'mp', axis=1, tiled=True)]
  transfers between devices with their start and end apart: 9 -> 3, of which waited for: 8 -> 3; matrix products, arithmetic and copies ran while one was open for 15% -> 0% of each run, Pallas kernels for 0% -> 0%
where the time goes in v1:
time: 664 us
  Pallas kernels  423 us (64%)
  waiting for transfers between devices  140 us (21%)
  matrix products  58.5 us (9%)
  other arithmetic  15.8 us (2%)
  between operations  14.6 us (2%)
  local copies, waits for them, and re-layouts  10.7 us (2%)
    pallas_call x1, Pallas kernels, attend_and_gather(): pl.pallas_call(functools.partial(attention_kernel, n, n_pairs, n_blocks),...  335 us
    pallas_call x1, Pallas kernels, gather_first(): pl.pallas_call(functools.partial(first_kernel, n, n_mp), out_shape=(jax.S...  88.4 us
    reduce_scatter x1, waiting for transfers between devices, on_device(): lax.psum_scatter(partial_value.astype(jnp.bfloat16), 'mp', scatter_dimens...  61.2 us
    reduce_scatter x1, waiting for transfers between devices, on_device(): lax.psum_scatter(terms.astype(jnp.bfloat16), 'mp', scatter_dimension=1, t...  44.7 us
    all_gather x1, waiting for transfers between devices, on_device(): mid_full = lax.all_gather(mid_local, 'mp', axis=1, tiled=True)  34.4 us
    dot_general x1, matrix products, on_device(): terms = jnp.dot(units, w_down_full, preferred_element_type=jnp.float32)  27.4 us
    dot_general x1, matrix products, on_device(): gate = jnp.dot(columns, w_gate_full, preferred_element_type=jnp.float32)  14.6 us
  transfers between devices with their start and end apart: 3, of which 3 were waited for; matrix products, arithmetic and copies ran while one was open for 0% of the time, Pallas kernels for 0%

profile of v1, /device:TPU:0, one launch (start us, length us, event | category | flops | bytes accessed | tf_op | source)
XLA Modules:
  0.0 663.6 jit_solution(14011271830504639016)
XLA Ops:
  7.2 0.7 convert_element_type.67
  7.9 88.4 %shard_map.130 = (bf16[1024,2048]{1,0:T(8,128)(2,1)}, bf16[3,2048,512]{2,1,0:T(8,128)(2,1)}) custom-call(bf16[1024,512]{1,0:T(8,128)(2,1)} %hid.1, bf16[3,256,512]{2,1,0:T(8,128)(2,1)} %wqkv.1), custom_call_target="tpu_custom_call" | custom-call | tf_op jit(solution)/shard_map/pallas_call | solution.py:142
  96.3 3.1 fusion
  99.4 10.5 %fusion.14 = f32[3,1024,512]{2,1,0:T(8,128)S(1)} fusion(bf16[3,2048,512]{2,1,0:T(8,128)(2,1)} %get-tuple-element.10, bf16[1024,2048]{1,0:T(8,128)(2,1)} %get-tuple-element.11, f32[2048]{0:T(1024)S(1)} %convert_element_type.67, f32[1024]{0:T(1024)S(1)} %add_rsqrt_fusion.1), kind=kOutput, calls=%fused_computation.19 | convolution fusion | flops 6450839552 | bytes 16789504 | tf_op jit(solution)/shard_map/nd,kdw->knw/dot_general | solution.py:288
  110.1 2.5 fusion.23
  113.2 1.9 copy.19
  115.1 2.9 copy.18
  118.0 0.5 multiply_cosine_fusion
  118.6 2.2 subtract_convert_fusion
  120.8 1.2 pad_maximum_fusion
  122.0 0.5 copy.20.q_ref
  122.5 1.5 copy.21.kn_ref
  124.1 1.2 copy-done.2
  125.3 335.1 %shard_map.131 = (bf16[1024,512]{1,0:T(8,128)(2,1)S(1)}, bf16[512,2048]{1,0:T(8,128)(2,1)}, bf16[2048,2048]{1,0:T(8,128)(2,1)}, bf16[2048,2048]{1,0:T(8,128)(2,1)}, bf16[2048,2048]{1,0:T(8,128)(2,1)}) custom-call(s32[1]{0:T(128)} %copy.25.length_ref, bf16[1024,512]{1,0:T(8,128)(2,1)S(1)} %copy.20.q_ref, bf16[1024,512]{1,0:T(8,128)(2,1)S(1)} %copy.21.kn_ref, ...), custom_call_target="tpu_custom_call" | custom-call | tf_op jit(solution)/shard_map/pallas_call | solution.py:260
  460.4 6.0 convolution_convert_fusion
  466.5 61.2 %reduce-scatter.3.cloned.1.call-done = bf16[1024,512]{1,0:T(8,128)(2,1)} async-done(((bf16[1024,2048]{1,0:T(8,128)(2,1)}), bf16[1024,512]{1,0:T(8,128)(2,1)}) %reduce-scatter.3.cloned.1.call-update) | async-done | bytes 1048592 | tf_op jit(solution)/shard_map/reduce_scatter | solution.py:309
  527.7 2.5 add_convert_fusion.1
  530.2 0.2 reduce-scatter.5.cloned.1.call-start
  530.4 34.4 %all-gather.2.cloned.1.call-done = bf16[1024,2048]{1,0:T(8,128)(2,1)} async-done(((bf16[1024,512]{1,0:T(8,128)(2,1)}), bf16[1024,2048]{1,0:T(8,128)(2,1)}) %all-gather.2.cloned.1.call-update) | async-done | bytes 4194320 | tf_op jit(solution)/shard_map/all_gather | solution.py:313
  564.8 3.1 fusion.3
  567.9 14.6 %fusion.19 = f32[1024,2048]{1,0:T(8,128)} fusion(bf16[2048,2048]{1,0:T(8,128)(2,1)} %get-tuple-element.14, bf16[1024,2048]{1,0:T(8,128)(2,1)} %all-gather.2.cloned.1.call-done, f32[2048]{0:T(1024)S(1)} %convert_element_type.78, f32[1024]{0:T(1024)S(1)} %add_rsqrt_fusion), kind=kOutput, calls=%fused_computation.23 | convolution fusion | flops 8598323200 | bytes 20983808 | tf_op jit(solution)/shard_map/dot_general | solution.py:316
  582.5 27.4 %fusion.13 = bf16[1024,2048]{1,0:T(8,128)(2,1)} fusion(bf16[2048,2048]{1,0:T(8,128)(2,1)} %get-tuple-element.16, f32[1024,2048]{1,0:T(8,128)} %fusion.19, bf16[2048,2048]{1,0:T(8,128)(2,1)} %get-tuple-element.15, bf16[1024,2048]{1,0:T(8,128)(2,1)} %all-gather.2.cloned.1.call-done, f32[2048]{0:T(1024)S(1)} %convert_element_type.78, f32[1024]{0:T(1024)S(1)} %add_rsqrt_fusion), kind=kOutput, calls=%fused_computation.18 | convolution fusion | flops 17202937856 | bytes 33566720 | tf_op jit(solution)/shard_map/dot_general | solution.py:325
  609.9 44.7 %reduce-scatter.5.cloned.1.call-done = bf16[1024,512]{1,0:T(8,128)(2,1)} async-done(((bf16[1024,2048]{1,0:T(8,128)(2,1)}), bf16[1024,512]{1,0:T(8,128)(2,1)}) %reduce-scatter.5.cloned.1.call-update) | async-done | bytes 1048592 | tf_op jit(solution)/shard_map/reduce_scatter | solution.py:328
  654.6 2.5 add_convert_fusion
  (24 shorter events, 0.3 us)
Async XLA Ops:
  7.2 520.5 %reduce-scatter.3.cloned.1.call-start = ((), (), s32[]{:S(2)}) async-start(), calls=%async_computation.2 | async-start | bytes 5242880 | tf_op jit(solution)/shard_map/reduce_scatter | solution.py:309
  110.0 14.0 %copy-start = (bf16[1024,512]{1,0:T(8,128)(2,1)}, bf16[1024,512]{1,0:T(8,128)(2,1)S(1)}, u32[]{:S(2)}) copy-start(bf16[1024,512]{1,0:T(8,128)(2,1)S(1)} %fusion.21.vn_ref) | copy-start | bytes 3145732
  118.6 5.5 copy-start.3
  124.1 1.2 copy-start.2
  125.3 335.1 %copy-start.1 = (bf16[1024,512]{1,0:T(8,128)(2,1)}, bf16[1024,512]{1,0:T(8,128)(2,1)S(1)}, u32[]{:S(2)}) copy-start(bf16[1024,512]{1,0:T(8,128)(2,1)S(1)} %copy.21.kn_ref) | copy-start | bytes 3145732
  460.4 67.3 %copy-start.5 = (bf16[1024,512]{1,0:T(8,128)(2,1)S(1)}, bf16[1024,512]{1,0:T(8,128)(2,1)}, u32[]{:S(2)}) copy-start(bf16[1024,512]{1,0:T(8,128)(2,1)} %hid.1) | copy-start | bytes 3145732
  466.4 64.0 %copy-start.6 = (bf16[2048]{0:T(1024)(128)(2,1)S(1)}, bf16[2048]{0:T(1024)(128)(2,1)}, u32[]{:S(2)}) copy-start(bf16[2048]{0:T(1024)(128)(2,1)} %param.15) | copy-start | bytes 12292
  466.4 98.4 %all-gather.2.cloned.1.call-start = ((), (), s32[]{:S(2)}) async-start(), calls=%async_computation.3 | async-start | bytes 5242880 | tf_op jit(solution)/shard_map/all_gather | solution.py:313
  530.2 124.4 %reduce-scatter.5.cloned.1.call-start = ((), (), s32[]{:S(2)}) async-start(), calls=%async_computation.4 | async-start | bytes 5242880 | tf_op jit(solution)/shard_map/reduce_scatter | solution.py:328
  582.5 72.1 %copy-start.4 = (bf16[1024,512]{1,0:T(8,128)(2,1)S(1)}, bf16[1024,512]{1,0:T(8,128)(2,1)}, u32[]{:S(2)}) copy-start(bf16[1024,512]{1,0:T(8,128)(2,1)} %add_convert_fusion.1) | copy-start | bytes 3145732
Sparse Core Ops, SparseCore 0:
  466.5 61.0 reduce-scatter.2
  530.3 34.4 all-gather.1
  610.0 44.5 reduce-scatter.4

commit v2 on v1

--- a/solution.py
+++ b/solution.py
@@ -40,12 +40,13 @@
     return ref.at[:, pl.ds(pl.multiple_of(index * width, width), width)]
 
 
-class ReqGather:
-    def __init__(self, n, pieces, sems):
+class Gather:
+    def __init__(self, axis, n, pieces, sems):
+        self.axis = axis
         self.half = n // 2
         self.pieces = pieces
         self.send_far, self.recv_far, self.send_near, self.recv_near, self.own_sem = sems
-        me = lax.axis_index("req")
+        me = lax.axis_index(axis)
         self.group, self.parity = me // 2, lax.rem(me, 2)
         self.me, self.partner = me, me + 1 - 2 * self.parity
 
@@ -54,22 +55,22 @@
 
     def greet(self, barrier):
         for shift in range(1, self.half):
-            pl.semaphore_signal(barrier, inc=1, device_id={"req": self.member(shift)}, device_id_type=MESH)
-        pl.semaphore_signal(barrier, inc=1, device_id={"req": self.partner}, device_id_type=MESH)
+            pl.semaphore_signal(barrier, inc=1, device_id={self.axis: self.member(shift)}, device_id_type=MESH)
+        pl.semaphore_signal(barrier, inc=1, device_id={self.axis: self.partner}, device_id_type=MESH)
         return self.half
 
     def far(self, c, shift):
         src, slot = self.pieces[c]
         return pltpu.make_async_remote_copy(
             src_ref=src, dst_ref=slot(self.me), send_sem=self.send_far.at[c, shift],
-            recv_sem=self.recv_far.at[c, shift], device_id={"req": self.member(shift)}, device_id_type=MESH)
+            recv_sem=self.recv_far.at[c, shift], device_id={self.axis: self.member(shift)}, device_id_type=MESH)
 
     def near(self, c, shift):
         src, slot = self.pieces[c]
         owner = self.member(-shift)
         return pltpu.make_async_remote_copy(
             src_ref=src if shift == 0 else slot(owner), dst_ref=slot(owner), send_sem=self.send_near.at[c, shift],
-            recv_sem=self.recv_near.at[c, shift], device_id={"req": self.partner}, device_id_type=MESH)
+            recv_sem=self.recv_near.at[c, shift], device_id={self.axis: self.partner}, device_id_type=MESH)
 
     def own(self, c):
         src, slot = self.pieces[c]
@@ -79,7 +80,8 @@
         for shift in range(1, self.half):
             self.far(c, shift).start()
         self.near(c, 0).start()
-        self.own(c).start()
+        if self.own_sem is not None:
+            self.own(c).start()
 
     def forward(self, c):
         for shift in range(1, self.half):
@@ -91,7 +93,8 @@
             self.far(c, shift).wait_send()
         for shift in range(self.half):
             self.near(c, shift).wait()
-        self.own(c).wait()
+        if self.own_sem is not None:
+            self.own(c).wait()
 
 
 def gather_sems(pieces, n):
@@ -106,7 +109,7 @@
         (wqkv.at[i], lambda r, i=i: wqkv_full.at[i, pl.ds(pl.multiple_of(r * depth, depth), depth)])
         for i in range(3)
     ]
-    gather = ReqGather(n, pieces, sems[:5])
+    gather = Gather("req", n, pieces, sems[:5])
     me = lax.axis_index("mp")
     barrier = pltpu.get_barrier_semaphore()
     expected = gather.greet(barrier)
@@ -202,8 +205,8 @@
 
 
 def attention_kernel(
-    n, n_pairs, n_blocks, length_ref, q_ref, kn_ref, vn_ref, kc_ref, vc_ref, w_out, w_gate, w_up, w_down,
-    out_ref, w_out_full, w_gate_full, w_up_full, w_down_full, *sems
+    n, n_pairs, n_blocks, length_ref, q_ref, kn_ref, vn_ref, kc_ref, vc_ref, w_out, w_gate, w_up,
+    out_ref, w_out_full, w_gate_full, w_up_full, *sems
 ):
     step = pl.program_id(0) * n_blocks + pl.program_id(1)
     steps = n_pairs * n_blocks
@@ -216,13 +219,7 @@
                 src.at[pl.ds(part * rows, rows)],
                 lambda r, full=full, part=part, depth=depth, rows=rows: full.at[
                     pl.ds(pl.multiple_of(r * depth + part * rows, rows), rows)]))
-    for part in range(2):
-        rows, width = w_down.shape[0] // 2, w_down.shape[1]
-        pieces.append((
-            w_down.at[pl.ds(part * rows, rows)],
-            lambda r, part=part, rows=rows, width=width: w_down_full.at[
-                pl.ds(part * rows, rows), pl.ds(pl.multiple_of(r * width, width), width)]))
-    gather = ReqGather(n, pieces, sems)
+    gather = Gather("req", n, pieces, sems)
     count = len(pieces)
 
     @pl.when(step == 0)
@@ -248,7 +245,7 @@
             gather.finish(c)
 
 
-def attend_and_gather(n, length, queries, keys, values, k_cache, v_cache, w_out, w_gate, w_up, w_down):
+def attend_and_gather(n, length, queries, keys, values, k_cache, v_cache, w_out, w_gate, w_up):
     rows, width = queries.shape
     slots = k_cache.shape[1]
     n_pairs, n_blocks = width // PAIR, 2
@@ -265,15 +262,236 @@
             like((w_out.shape[0], w_out.shape[1] * n), w_out.dtype),
             like((w_gate.shape[0] * n, w_gate.shape[1]), w_gate.dtype),
             like((w_up.shape[0] * n, w_up.shape[1]), w_up.dtype),
-            like((w_down.shape[0], w_down.shape[1] * n), w_down.dtype),
         ),
-        in_specs=[pl.BlockSpec(memory_space=pltpu.SMEM), row_block, whole, whole, cached, cached] + [hbm] * 4,
-        out_specs=(row_block,) + (hbm,) * 4,
-        scratch_shapes=gather_sems(7, n),
+        in_specs=[pl.BlockSpec(memory_space=pltpu.SMEM), row_block, whole, whole, cached, cached] + [hbm] * 3,
+        out_specs=(row_block,) + (hbm,) * 3,
+        scratch_shapes=gather_sems(5, n),
         compiler_params=pltpu.CompilerParams(
             collective_id=1, has_side_effects=True, vmem_limit_bytes=48 * 1024 * 1024,
             dimension_semantics=("arbitrary", "arbitrary")),
-    )(length, queries, keys, values, k_cache, v_cache, w_out, w_gate, w_up, w_down)
+    )(length, queries, keys, values, k_cache, v_cache, w_out, w_gate, w_up)
+
+
+CHUNKS = 4
+DOWN_PIECES = 4
+
+
+class Reduce:
+    def __init__(self, n, part, near_in, far_out, far_in, sems):
+        self.half, self.part, self.near_in, self.far_out, self.far_in = n // 2, part, near_in, far_out, far_in
+        self.near_send, self.near_recv, self.far_send, self.far_recv = sems
+        self.me = lax.axis_index("mp")
+        self.group, self.parity = self.me // 2, lax.rem(self.me, 2)
+        self.partner = self.me + 1 - 2 * self.parity
+        self.width = part.shape[1] // n
+        self.rows = part.shape[0] // CHUNKS
+
+    def rows_of(self, c):
+        return pl.ds(c * self.rows, self.rows)
+
+    def block(self, c, index):
+        return self.part.at[
+            self.rows_of(c), pl.ds(pl.multiple_of(index * self.width, self.width), self.width)]
+
+    def near(self, c, g):
+        return pltpu.make_async_remote_copy(
+            src_ref=self.block(c, g * 2 + 1 - self.parity), dst_ref=self.near_in.at[g, self.rows_of(c)],
+            send_sem=self.near_send.at[c, g], recv_sem=self.near_recv.at[c, g],
+            device_id={"mp": self.partner}, device_id_type=MESH)
+
+    def far(self, c, shift):
+        target = lax.rem(self.group + shift, self.half)
+        return pltpu.make_async_remote_copy(
+            src_ref=self.far_out.at[shift, self.rows_of(c)], dst_ref=self.far_in.at[shift, self.rows_of(c)],
+            send_sem=self.far_send.at[c, shift], recv_sem=self.far_recv.at[c, shift],
+            device_id={"mp": target * 2 + self.parity}, device_id_type=MESH)
+
+    def start(self, c):
+        for g in range(self.half):
+            self.near(c, g).start()
+
+    def pair_sum(self, c, group):
+        return self.block(c, group * 2 + self.parity)[...].astype(jnp.float32) + self.near_in[
+            group, self.rows_of(c)].astype(jnp.float32)
+
+    def send_sums(self, c):
+        for g in range(self.half):
+            self.near(c, g).wait_recv()
+        for shift in range(1, self.half):
+            target = lax.rem(self.group + shift, self.half)
+            self.far_out[shift, self.rows_of(c)] = self.pair_sum(c, target).astype(jnp.bfloat16)
+            self.far(c, shift).start()
+
+    def total(self, c):
+        value = self.pair_sum(c, self.group)
+        for shift in range(1, self.half):
+            self.far(c, shift).wait_recv()
+            value = value + self.far_in[shift, self.rows_of(c)].astype(jnp.float32)
+        return value
+
+    def finish(self, c):
+        for g in range(self.half):
+            self.near(c, g).wait_send()
+        for shift in range(1, self.half):
+            self.far(c, shift).wait_send()
+
+
+def reduce_scratch(rows, width, n):
+    dma = pltpu.SemaphoreType.DMA((CHUNKS, n // 2))
+    buffers = [pltpu.VMEM((rows, width * n), jnp.bfloat16)] + [
+        pltpu.VMEM((n // 2, rows, width), jnp.bfloat16) for _ in range(3)]
+    return buffers + [dma] * 4
+
+
+def dot_tiles(left, right, out, rows):
+    columns = out.shape[1]
+    tile = min(columns, 512)
+
+    @pl.loop(0, columns // tile)
+    def _(index):
+        cols = pl.ds(pl.multiple_of(index * tile, tile), tile)
+        out[rows, cols] = jnp.dot(
+            left[rows, :], right[:, cols], preferred_element_type=jnp.float32).astype(out.dtype)
+
+
+def middle_kernel(
+    n, n_mp, attn, w_out, hidden, gain, w_gate, w_up, w_down, mid_out, units, w_down_full,
+    normed, mid_full, part, near_in, far_out, far_in, *sems
+):
+    rows, width = hidden.shape
+    step = rows // CHUNKS
+    piece_rows, piece_width = w_down.shape[0] // DOWN_PIECES, w_down.shape[1]
+    pieces = [
+        (w_down.at[pl.ds(p * piece_rows, piece_rows)],
+         lambda r, p=p: w_down_full.at[
+             pl.ds(p * piece_rows, piece_rows), pl.ds(pl.multiple_of(r * piece_width, piece_width), piece_width)])
+        for p in range(DOWN_PIECES)
+    ]
+    reduce = Reduce(n_mp, part, near_in, far_out, far_in, sems[:4])
+    me = reduce.me
+
+    def mid_block(c, r):
+        return mid_full.at[pl.ds(c * step, step), pl.ds(pl.multiple_of(r * width, width), width)]
+
+    down = Gather("req", n, pieces, sems[4:9])
+    spread = Gather(
+        "mp", n_mp, [(mid_block(c, me), lambda r, c=c: mid_block(c, r)) for c in range(CHUNKS)],
+        sems[9:13] + (None,))
+    barrier = pltpu.get_barrier_semaphore()
+    pl.semaphore_wait(barrier, down.greet(barrier) + spread.greet(barrier))
+    for p in range(2):
+        down.start(p)
+
+    def chunk_rows(c):
+        return pl.ds(c * step, step)
+
+    def mid_chunk(c):
+        value = (hidden[chunk_rows(c)].astype(jnp.float32) + reduce.total(c)).astype(jnp.bfloat16)
+        mid_block(c, me)[...] = value
+        mid_out[chunk_rows(c)] = value
+        spread.start(c)
+
+    for c in range(CHUNKS + 3):
+        if c < CHUNKS:
+            dot_tiles(attn, w_out, part, chunk_rows(c))
+            reduce.start(c)
+        if 1 <= c <= CHUNKS:
+            reduce.send_sums(c - 1)
+        if 2 <= c <= CHUNKS + 1:
+            mid_chunk(c - 2)
+        if 3 <= c:
+            spread.forward(c - 3)
+    down.forward(0)
+    down.start(2)
+    columns = units.shape[1]
+    tile = min(columns, 512)
+    for c in range(CHUNKS):
+        for shift in range(spread.half):
+            spread.near(c, shift).wait_recv()
+        values = mid_full[chunk_rows(c)].astype(jnp.float32)
+        meansq = jnp.mean(values * values, axis=-1, keepdims=True)
+        normed[...] = (values * lax.rsqrt(meansq + EPSILON) * gain[...].astype(jnp.float32)).astype(jnp.bfloat16)
+
+        @pl.loop(0, columns // tile)
+        def _(index, c=c):
+            cols = pl.ds(pl.multiple_of(index * tile, tile), tile)
+            gate = jnp.dot(normed[...], w_gate[:, cols], preferred_element_type=jnp.float32)
+            upper = jnp.dot(normed[...], w_up[:, cols], preferred_element_type=jnp.float32)
+            units[chunk_rows(c), cols] = (gate * jax.nn.sigmoid(gate) * upper).astype(units.dtype)
+
+        if c == 1:
+            down.forward(1)
+            down.start(3)
+    for p in range(2, DOWN_PIECES):
+        down.forward(p)
+    for c in range(CHUNKS):
+        reduce.finish(c)
+        for shift in range(1, spread.half):
+            spread.far(c, shift).wait_send()
+        for shift in range(spread.half):
+            spread.near(c, shift).wait_send()
+    for p in range(DOWN_PIECES):
+        down.finish(p)
+
+
+def middle(n, n_mp, attn, w_out_full, hidden_in, gain, w_gate_full, w_up_full, w_down):
+    rows, width = hidden_in.shape
+    features = width * n_mp
+    vmem, hbm = pl.BlockSpec(memory_space=pltpu.VMEM), pl.BlockSpec(memory_space=pl.ANY)
+    like, bf16 = jax.ShapeDtypeStruct, jnp.bfloat16
+    dma = pltpu.SemaphoreType.DMA
+    return pl.pallas_call(
+        functools.partial(middle_kernel, n, n_mp),
+        out_shape=(
+            like((rows, width), bf16),
+            like((rows, w_gate_full.shape[1]), bf16),
+            like((w_down.shape[0], w_down.shape[1] * n), bf16),
+        ),
+        in_specs=[vmem] * 6 + [hbm],
+        out_specs=(vmem, vmem, hbm),
+        scratch_shapes=[pltpu.VMEM((rows // CHUNKS, features), bf16), pltpu.VMEM((rows, features), bf16)]
+        + reduce_scratch(rows, width, n_mp) + gather_sems(DOWN_PIECES, n)
+        + [dma((CHUNKS, n_mp // 2)) for _ in range(4)],
+        compiler_params=pltpu.CompilerParams(
+            collective_id=2, has_side_effects=True, vmem_limit_bytes=56 * 1024 * 1024),
+    )(attn, w_out_full, hidden_in, gain.reshape(1, features), w_gate_full, w_up_full, w_down)
+
+
+def last_kernel(n_mp, units, w_down, mid, out, part, near_in, far_out, far_in, *sems):
+    rows = mid.shape[0]
+    step = rows // CHUNKS
+    reduce = Reduce(n_mp, part, near_in, far_out, far_in, sems)
+    barrier = pltpu.get_barrier_semaphore()
+    for shift in range(1, reduce.half):
+        target = lax.rem(reduce.group + shift, reduce.half) * 2 + reduce.parity
+        pl.semaphore_signal(barrier, inc=1, device_id={"mp": target}, device_id_type=MESH)
+    pl.semaphore_signal(barrier, inc=1, device_id={"mp": reduce.partner}, device_id_type=MESH)
+    pl.semaphore_wait(barrier, reduce.half)
+    for c in range(CHUNKS + 2):
+        if c < CHUNKS:
+            dot_tiles(units, w_down, part, pl.ds(c * step, step))
+            reduce.start(c)
+        if 1 <= c <= CHUNKS:
+            reduce.send_sums(c - 1)
+        if 2 <= c:
+            chunk = pl.ds((c - 2) * step, step)
+            out[chunk] = (mid[chunk].astype(jnp.float32) + reduce.total(c - 2)).astype(out.dtype)
+    for c in range(CHUNKS):
+        reduce.finish(c)
+
+
+def last(n_mp, units, w_down_full, mid):
+    rows, width = mid.shape
+    vmem = pl.BlockSpec(memory_space=pltpu.VMEM)
+    return pl.pallas_call(
+        functools.partial(last_kernel, n_mp),
+        out_shape=jax.ShapeDtypeStruct((rows, width), jnp.bfloat16),
+        in_specs=[vmem] * 3,
+        out_specs=vmem,
+        scratch_shapes=reduce_scratch(rows, width, n_mp),
+        compiler_params=pltpu.CompilerParams(
+            collective_id=3, has_side_effects=True, vmem_limit_bytes=48 * 1024 * 1024),
+    )(units, w_down_full, mid)
 
 
 def on_device(
@@ -300,35 +518,12 @@
         jnp.bfloat16
     )
     fresh_values = projected[2].astype(jnp.bfloat16).reshape(new_count, heads_local, HD)
-    attn, w_out_full, w_gate_full, w_up_full, w_down_full = attend_and_gather(
+    attn, w_out_full, w_gate_full, w_up_full = attend_and_gather(
         n, cache_len, queries.reshape(new_count, width), fresh_keys.reshape(new_count, width),
-        fresh_values.reshape(new_count, width), k_cache, v_cache, w_out, w_gate, w_up, w_down)
-    partial_value = jnp.dot(
-        attn, w_out_full, preferred_element_type=jnp.float32
-    )
-    summed = lax.psum_scatter(
-        partial_value.astype(jnp.bfloat16), "mp", scatter_dimension=1, tiled=True
-    ).astype(jnp.float32)
-    mid_local = (hidden_in.astype(jnp.float32) + summed).astype(jnp.bfloat16)
-    mid_full = lax.all_gather(mid_local, "mp", axis=1, tiled=True)
-    normed2 = rms_scale(mid_full, mlp_gain)
-    columns = normed2
-    gate = jnp.dot(
-        columns,
-        w_gate_full,
-        preferred_element_type=jnp.float32,
-    )
-    upper = jnp.dot(
-        columns, w_up_full, preferred_element_type=jnp.float32
-    )
-    units = (jax.nn.silu(gate) * upper).astype(jnp.bfloat16)
-    terms = jnp.dot(
-        units, w_down_full, preferred_element_type=jnp.float32
-    )
-    reduced = lax.psum_scatter(
-        terms.astype(jnp.bfloat16), "mp", scatter_dimension=1, tiled=True
-    ).astype(jnp.float32)
-    hidden_out = (mid_local.astype(jnp.float32) + reduced).astype(jnp.bfloat16)
+        fresh_values.reshape(new_count, width), k_cache, v_cache, w_out, w_gate, w_up)
+    mid_local, units, w_down_full = middle(
+        n, n_mp, attn, w_out_full, hidden_in, mlp_gain, w_gate_full, w_up_full, w_down)
+    hidden_out = last(n_mp, units, w_down_full, mid_local)
     return (
         hidden_out,
         fresh_keys.reshape(new_count, width),

time: 664 us -> 556 us (0.84)
  waiting for transfers between devices: 140 us -> 0 us
  Pallas kernels: 423 us -> 522 us
  matrix products: 58.5 us -> 9.32 us
  between operations: 14.6 us -> 1.45 us
  other arithmetic: 15.8 us -> 7.83 us
    pallas_call x0 -> x2, Pallas kernels: none -> 189 us  [the longest x1 153 us: middle(): pl.pallas_call(functools.partial(middle_kernel, n, n_mp), out_shape=(like...]
    reduce_scatter x2 -> x0, waiting for transfers between devices: 106 us -> none  [the longest x1 61.2 us: on_device(): lax.psum_scatter(partial_value.astype(jnp.bfloat16), 'mp', scatter_dimens...]
    pallas_call x1, Pallas kernels: 335 us -> 245 us  [attend_and_gather(): pl.pallas_call(functools.partial(attention_kernel, n, n_pairs, n_blocks),...]
    dot_general x3 -> x0, matrix products: 48 us -> none  [the longest x1 27.4 us: on_device(): terms = jnp.dot(units, w_down_full, preferred_element_type=jnp.float32)]
    all_gather x1 -> x0, waiting for transfers between devices: 34.4 us -> none  [on_device(): mid_full = lax.all_gather(mid_local, 'mp', axis=1, tiled=True)]
  transfers between devices with their start and end apart: 3 -> 0, of which waited for: 3 -> 0; matrix products, arithmetic and copies ran while one was open for 0% -> 0% of each run, Pallas kernels for 0% -> 0%
where the time goes in v2:
time: 556 us
  Pallas kernels  522 us (94%)
  local copies, waits for them, and re-layouts  15.3 us (3%)
  matrix products  9.32 us (2%)
  other arithmetic  7.83 us (1%)
    pallas_call x1, Pallas kernels, attend_and_gather(): pl.pallas_call(functools.partial(attention_kernel, n, n_pairs, n_blocks),...  245 us
    pallas_call x1, Pallas kernels, middle(): pl.pallas_call(functools.partial(middle_kernel, n, n_mp), out_shape=(like...  153 us
    pallas_call x1, Pallas kernels, gather_first(): pl.pallas_call(functools.partial(first_kernel, n, n_mp), out_shape=(jax.S...  88.5 us
    pallas_call x1, Pallas kernels, last(): pl.pallas_call(functools.partial(last_kernel, n_mp), out_shape=jax.ShapeD...  35.5 us

profile of v2, /device:TPU:0, one launch (start us, length us, event | category | flops | bytes accessed | tf_op | source)
XLA Modules:
  0.0 555.8 jit_solution(3420783877057730820)
XLA Ops:
  1.3 0.7 convert_element_type.30
  2.0 1.3 reshape.95.gain
  3.3 0.5 multiply_cosine_fusion
  3.8 88.5 %shard_map.130 = (bf16[1024,2048]{1,0:T(8,128)(2,1)}, bf16[3,2048,512]{2,1,0:T(8,128)(2,1)}) custom-call(bf16[1024,512]{1,0:T(8,128)(2,1)} %hidden.1, bf16[3,256,512]{2,1,0:T(8,128)(2,1)} %wqkv.1), custom_call_target="tpu_custom_call" | custom-call | tf_op jit(solution)/shard_map/pallas_call | solution.py:145
  92.3 3.2 fusion
  95.5 0.2 copy-done.6
  95.7 9.3 %fusion.8 = f32[3,1024,512]{2,1,0:T(8,128)S(1)} fusion(bf16[3,2048,512]{2,1,0:T(8,128)(2,1)} %get-tuple-element.12, bf16[1024,2048]{1,0:T(8,128)(2,1)S(1)} %copy-done.6, f32[2048]{0:T(1024)S(1)} %convert_element_type.30, f32[1024]{0:T(1024)S(1)} %add_rsqrt_fusion), kind=kOutput, calls=%fused_computation.9 | convolution fusion | flops 6450839552 | bytes 16789504 | tf_op jit(solution)/shard_map/nd,kdw->knw/dot_general | solution.py:506
  105.1 0.1 fusion.11.vn_ref
  105.2 0.0 copy-start
  105.2 2.5 fusion.12
  107.7 1.9 copy.19
  109.6 2.9 copy.18
  112.5 2.2 subtract_convert_fusion
  114.7 0.0 copy-start.5
  114.7 1.2 pad_maximum_fusion
  115.9 0.5 copy.20.q_ref
  116.5 1.5 copy.21.kn_ref
  118.0 1.2 copy-done.4
  119.2 244.8 %shard_map.131 = (bf16[1024,512]{1,0:T(8,128)(2,1)S(1)}, bf16[512,2048]{1,0:T(8,128)(2,1)}, bf16[2048,2048]{1,0:T(8,128)(2,1)}, bf16[2048,2048]{1,0:T(8,128)(2,1)}) custom-call(s32[1]{0:T(128)} %copy.26.length_ref, bf16[1024,512]{1,0:T(8,128)(2,1)S(1)} %copy.20.q_ref, bf16[1024,512]{1,0:T(8,128)(2,1)S(1)} %copy.21.kn_ref, ...), custom_call_target="tpu_custom_call" | custom-call | tf_op jit(solution)/shard_map/pallas_call | solution.py:257
  364.0 1.0 copy-done.3
  365.0 153.1 %shard_map.132 = (bf16[1024,512]{1,0:T(8,128)(2,1)}, bf16[1024,2048]{1,0:T(8,128)(2,1)}, bf16[2048,2048]{1,0:T(8,128)(2,1)}) custom-call(bf16[1024,512]{1,0:T(8,128)(2,1)} %copy-done.3, bf16[512,2048]{1,0:T(8,128)(2,1)} %get-tuple-element.15.w_out, bf16[1024,512]{1,0:T(8,128)(2,1)} %hidden.1, bf16[1,2048]{1,0:T(2,128)(2,1)} %reshape.95.gain, ...), custom_call_target="tpu_custom_call" | custom-call | tf_op jit(solution)/shard_map/pallas_call | solution.py:443
  518.1 1.2 copy-done.2
  519.3 35.5 %shard_map.133 = bf16[1024,512]{1,0:T(8,128)(2,1)S(1)} custom-call(bf16[1024,2048]{1,0:T(8,128)(2,1)} %get-tuple-element.18.units, bf16[2048,2048]{1,0:T(8,128)(2,1)} %get-tuple-element.19.w_down, bf16[1024,512]{1,0:T(8,128)(2,1)S(1)} %copy-done.2), custom_call_target="tpu_custom_call" | custom-call | tf_op jit(solution)/shard_map/pallas_call | solution.py:486
  554.9 1.0 copy.27
  (11 shorter events, 0.0 us)
Async XLA Ops:
  92.3 3.5 copy-start.6
  105.2 12.8 %copy-start = (bf16[1024,512]{1,0:T(8,128)(2,1)}, bf16[1024,512]{1,0:T(8,128)(2,1)S(1)}, u32[]{:S(2)}) copy-start(bf16[1024,512]{1,0:T(8,128)(2,1)S(1)} %fusion.11.vn_ref) | copy-start | bytes 3145732
  114.7 3.3 copy-start.5
  118.0 1.2 copy-start.4
  119.2 244.8 %copy-start.1 = (bf16[1024,512]{1,0:T(8,128)(2,1)}, bf16[1024,512]{1,0:T(8,128)(2,1)S(1)}, u32[]{:S(2)}) copy-start(bf16[1024,512]{1,0:T(8,128)(2,1)S(1)} %copy.21.kn_ref) | copy-start | bytes 3145732
  364.0 1.0 copy-start.3
  518.1 1.2 copy-start.2

commit v3 on v2

--- a/solution.py
+++ b/solution.py
@@ -17,23 +17,12 @@
 NEG_FILL = -1e30
 
 
-def rms_scale(rows, gain):
-    values = rows.astype(jnp.float32)
-    meansq = jnp.mean(values * values, axis=-1, keepdims=True)
-    return (values * lax.rsqrt(meansq + EPSILON) * gain.astype(jnp.float32)).astype(jnp.bfloat16)
-
-
-def rotate(tensor, positions):
-    half = tensor.shape[-1] // 2
-    freq = THETA ** (-(jnp.arange(half, dtype=jnp.float32) * 2.0 / tensor.shape[-1]))
-    angle = positions[:, None, None] * freq[None, None, :]
-    cosine = jnp.cos(angle)
-    sine = jnp.sin(angle)
-    first = tensor[..., :half]
-    second = tensor[..., half:]
-    return jnp.concatenate(
-        [first * cosine - second * sine, second * cosine + first * sine], axis=-1
-    )
+def rotation(positions):
+    half = HD // 2
+    freq = THETA ** (-(jnp.arange(half, dtype=jnp.float32) * 2.0 / HD))
+    angle = positions[:, None] * freq[None, :]
+    cosine, sine = jnp.cos(angle), jnp.sin(angle)
+    return jnp.tile(cosine, (1, 4)), jnp.tile(jnp.concatenate([-sine, sine], axis=1), (1, 2))
 
 
 def columns_of(ref, index, width):
@@ -105,9 +94,12 @@
 def first_kernel(n, n_mp, hid, wqkv, hid_full, wqkv_full, *sems):
     mp_send, mp_recv, mp_own = sems[5:]
     depth, width = wqkv.shape[1], hid.shape[1]
+    rows = depth // 2
     pieces = [
-        (wqkv.at[i], lambda r, i=i: wqkv_full.at[i, pl.ds(pl.multiple_of(r * depth, depth), depth)])
-        for i in range(3)
+        (wqkv.at[i, pl.ds(part * rows, rows)],
+         lambda r, i=i, part=part: wqkv_full.at[
+             i, pl.ds(pl.multiple_of(r * depth + part * rows, rows), rows)])
+        for i in range(3) for part in range(2)
     ]
     gather = Gather("req", n, pieces, sems[:5])
     me = lax.axis_index("mp")
@@ -124,14 +116,14 @@
         for shift in range(1, n_mp)
     ]
     own = pltpu.make_async_copy(hid, mine, mp_own)
-    for c in range(3):
+    for c in range(6):
         gather.start(c)
     for copy in copies:
         copy.start()
     own.start()
-    for c in range(3):
+    for c in range(6):
         gather.forward(c)
-    for c in range(3):
+    for c in range(6):
         gather.finish(c)
     for copy in copies:
         copy.wait()
@@ -150,19 +142,41 @@
         ),
         in_specs=[hbm, hbm],
         out_specs=(hbm, hbm),
-        scratch_shapes=gather_sems(3, n) + [dma((n_mp,)), dma((n_mp,)), dma],
+        scratch_shapes=gather_sems(6, n) + [dma((n_mp,)), dma((n_mp,)), dma],
         compiler_params=pltpu.CompilerParams(collective_id=0, has_side_effects=True),
     )(hidden_in, w_qkv)
 
 
-def attend(length, q_begin, q_ref, kn_ref, vn_ref, kc_ref, vc_ref, out_ref):
-    rows = q_ref.shape[0]
+def project(hidden, gain, w_qkv, cosine, sine, queries, keys, values):
+    rows, width = queries.shape
+    step = min(rows, 256)
+    lane = lax.broadcasted_iota(jnp.int32, (1, PAIR), 1)
+    first = lax.rem(lane, HD) < HD // 2
+
+    @pl.loop(0, rows // step)
+    def _(index):
+        chunk = pl.ds(pl.multiple_of(index * step, step), step)
+        entries = hidden[chunk, :].astype(jnp.float32)
+        meansq = jnp.mean(entries * entries, axis=-1, keepdims=True)
+        normed = (entries * lax.rsqrt(meansq + EPSILON) * gain[...].astype(jnp.float32)).astype(jnp.bfloat16)
+        for i, out in enumerate((queries, keys, values)):
+            product = jnp.dot(normed, w_qkv[i], preferred_element_type=jnp.float32)
+            for begin in range(0, width, PAIR):
+                part = product[:, begin : begin + PAIR]
+                if i < 2:
+                    other = jnp.where(first, pltpu.roll(part, PAIR - HD // 2, 1), pltpu.roll(part, HD // 2, 1))
+                    part = part * cosine[chunk, :] + other * sine[chunk, :]
+                out[chunk, begin : begin + PAIR] = part.astype(out.dtype)
+
+
+def attend(length, pair, q_begin, rows, q_ref, kn_ref, vn_ref, kc_ref, vc_ref, out_ref):
     fresh = kn_ref.shape[0]
     slots = kc_ref.shape[1]
     block = min(slots, 512)
     lane = lax.broadcasted_iota(jnp.int32, (1, PAIR), 1)
     masks = (lane < HD, lane >= HD)
-    query = q_ref[...]
+    cols = pl.ds(pl.multiple_of(pair * PAIR, PAIR), PAIR)
+    query = q_ref[pl.ds(pl.multiple_of(q_begin, rows), rows), cols]
     queries = [jnp.where(mask, query, 0) for mask in masks]
     row_index = q_begin + lax.broadcasted_iota(jnp.int32, (rows, 1), 0)
 
@@ -187,7 +201,7 @@
         begin = pl.multiple_of(index * block, block)
         column = begin + lax.broadcasted_iota(jnp.int32, (1, block), 1)
         return absorb(
-            state, kn_ref[pl.ds(begin, block)], vn_ref[pl.ds(begin, block)],
+            state, kn_ref[pl.ds(begin, block), cols], vn_ref[pl.ds(begin, block), cols],
             lambda scores: jnp.where(row_index >= column, scores, NEG_FILL))
 
     def cache_step(index, state):
@@ -204,76 +218,90 @@
     out_ref[...] = jnp.where(masks[0], parts[0], parts[1]).astype(out_ref.dtype)
 
 
+QUARTERS = 4
+PIECES = 1 + 2 * QUARTERS
+
+
 def attention_kernel(
-    n, n_pairs, n_blocks, length_ref, q_ref, kn_ref, vn_ref, kc_ref, vc_ref, w_out, w_gate, w_up,
-    out_ref, w_out_full, w_gate_full, w_up_full, *sems
+    n, n_pairs, n_blocks, length_ref, hidden, gain, w_qkv, cosine, sine, kc_ref, vc_ref, w_out, w_gate, w_up,
+    out_ref, keys, values, w_out_full, w_gate_full, w_up_full, queries, *sems
 ):
     step = pl.program_id(0) * n_blocks + pl.program_id(1)
     steps = n_pairs * n_blocks
     pieces = [(w_out, lambda r: columns_of(w_out_full, r, w_out.shape[1]))]
     for src, full in ((w_gate, w_gate_full), (w_up, w_up_full)):
         depth = src.shape[0]
-        for part in range(2):
-            rows = depth // 2
+        for part in range(QUARTERS):
+            rows = depth // QUARTERS
             pieces.append((
                 src.at[pl.ds(part * rows, rows)],
                 lambda r, full=full, part=part, depth=depth, rows=rows: full.at[
                     pl.ds(pl.multiple_of(r * depth + part * rows, rows), rows)]))
     gather = Gather("req", n, pieces, sems)
-    count = len(pieces)
 
     @pl.when(step == 0)
     def _():
         barrier = pltpu.get_barrier_semaphore()
         pl.semaphore_wait(barrier, gather.greet(barrier))
-        for c in range(3):
+        for c in range(PIECES):
             gather.start(c)
-
+        project(hidden, gain, w_qkv, cosine, sine, queries, keys, values)
+
+    rows = out_ref.shape[0]
     attend(
-        length_ref[0], pl.program_id(1) * q_ref.shape[0], q_ref, kn_ref, vn_ref, kc_ref, vc_ref, out_ref)
-
-    for c in range(count):
+        length_ref[0], pl.program_id(0), pl.program_id(1) * rows, rows, queries, keys, values, kc_ref, vc_ref,
+        out_ref)
+
+    for c in range(PIECES):
         @pl.when(step == min(c, steps - 1))
         def _(c=c):
             gather.forward(c)
-            if c + 3 < count:
-                gather.start(c + 3)
 
     @pl.when(step == steps - 1)
     def _():
-        for c in range(count):
+        for c in range(PIECES):
             gather.finish(c)
 
 
-def attend_and_gather(n, length, queries, keys, values, k_cache, v_cache, w_out, w_gate, w_up):
-    rows, width = queries.shape
+def attend_and_gather(n, length, hidden, gain, w_qkv, cosine, sine, k_cache, v_cache, w_out, w_gate, w_up):
+    rows, features = hidden.shape
+    width = w_qkv.shape[2]
     slots = k_cache.shape[1]
     n_pairs, n_blocks = width // PAIR, 2
     hbm = pl.BlockSpec(memory_space=pl.ANY)
     row_block = pl.BlockSpec((rows // n_blocks, PAIR), lambda h, i: (i, h))
-    whole = pl.BlockSpec((rows, PAIR), lambda h, i: (0, h))
     cached = pl.BlockSpec((1, slots, PAIR), lambda h, i: (0, 0, h))
-    like = jax.ShapeDtypeStruct
+
+    def whole(*shape):
+        return pl.BlockSpec(shape, lambda h, i: (0,) * len(shape), pipeline_mode=pl.Buffered(1))
+
+    fresh = pl.BlockSpec((rows, width), lambda h, i: (0, 0))
+    like, bf16 = jax.ShapeDtypeStruct, jnp.bfloat16
     return pl.pallas_call(
         functools.partial(attention_kernel, n, n_pairs, n_blocks),
         grid=(n_pairs, n_blocks),
         out_shape=(
-            like((rows, width), queries.dtype),
+            like((rows, width), bf16),
+            like((rows, width), bf16),
+            like((rows, width), bf16),
             like((w_out.shape[0], w_out.shape[1] * n), w_out.dtype),
             like((w_gate.shape[0] * n, w_gate.shape[1]), w_gate.dtype),
             like((w_up.shape[0] * n, w_up.shape[1]), w_up.dtype),
         ),
-        in_specs=[pl.BlockSpec(memory_space=pltpu.SMEM), row_block, whole, whole, cached, cached] + [hbm] * 3,
-        out_specs=(row_block,) + (hbm,) * 3,
-        scratch_shapes=gather_sems(5, n),
+        in_specs=[
+            pl.BlockSpec(memory_space=pltpu.SMEM), whole(rows, features), whole(1, features),
+            whole(*w_qkv.shape), whole(rows, PAIR), whole(rows, PAIR), cached, cached,
+        ] + [hbm] * 3,
+        out_specs=(row_block, fresh, fresh) + (hbm,) * 3,
+        scratch_shapes=[pltpu.VMEM((rows, width), bf16)] + gather_sems(PIECES, n),
         compiler_params=pltpu.CompilerParams(
-            collective_id=1, has_side_effects=True, vmem_limit_bytes=48 * 1024 * 1024,
+            collective_id=1, has_side_effects=True, vmem_limit_bytes=56 * 1024 * 1024,
             dimension_semantics=("arbitrary", "arbitrary")),
-    )(length, queries, keys, values, k_cache, v_cache, w_out, w_gate, w_up)
+    )(length, hidden, gain.reshape(1, features), w_qkv, cosine, sine, k_cache, v_cache, w_out, w_gate, w_up)
 
 
 CHUNKS = 4
-DOWN_PIECES = 4
+DOWN_PIECES = 8
 
 
 class Reduce:
@@ -355,8 +383,8 @@
 
 
 def middle_kernel(
-    n, n_mp, attn, w_out, hidden, gain, w_gate, w_up, w_down, mid_out, units, w_down_full,
-    normed, mid_full, part, near_in, far_out, far_in, *sems
+    n, n_mp, attn, w_out, hidden, gain, w_gate_full, w_up_full, w_down, mid_out, units, w_down_full,
+    gate_in, up_in, load_sems, normed, mid_full, part, near_in, far_out, far_in, *sems
 ):
     rows, width = hidden.shape
     step = rows // CHUNKS
@@ -379,8 +407,14 @@
         sems[9:13] + (None,))
     barrier = pltpu.get_barrier_semaphore()
     pl.semaphore_wait(barrier, down.greet(barrier) + spread.greet(barrier))
-    for p in range(2):
+    for p in range(DOWN_PIECES):
         down.start(p)
+    loads = [
+        pltpu.make_async_copy(w_gate_full, gate_in, load_sems.at[0]),
+        pltpu.make_async_copy(w_up_full, up_in, load_sems.at[1]),
+    ]
+    for load in loads:
+        load.start()
 
     def chunk_rows(c):
         return pl.ds(c * step, step)
@@ -401,8 +435,10 @@
             mid_chunk(c - 2)
         if 3 <= c:
             spread.forward(c - 3)
-    down.forward(0)
-    down.start(2)
+        if 2 <= c:
+            down.forward(c - 2)
+    for load in loads:
+        load.wait()
     columns = units.shape[1]
     tile = min(columns, 512)
     for c in range(CHUNKS):
@@ -415,15 +451,12 @@
         @pl.loop(0, columns // tile)
         def _(index, c=c):
             cols = pl.ds(pl.multiple_of(index * tile, tile), tile)
-            gate = jnp.dot(normed[...], w_gate[:, cols], preferred_element_type=jnp.float32)
-            upper = jnp.dot(normed[...], w_up[:, cols], preferred_element_type=jnp.float32)
+            gate = jnp.dot(normed[...], gate_in[:, cols], preferred_element_type=jnp.float32)
+            upper = jnp.dot(normed[...], up_in[:, cols], preferred_element_type=jnp.float32)
             units[chunk_rows(c), cols] = (gate * jax.nn.sigmoid(gate) * upper).astype(units.dtype)
 
-        if c == 1:
-            down.forward(1)
-            down.start(3)
-    for p in range(2, DOWN_PIECES):
-        down.forward(p)
+        if CHUNKS + 1 + c < DOWN_PIECES:
+            down.forward(CHUNKS + 1 + c)
     for c in range(CHUNKS):
         reduce.finish(c)
         for shift in range(1, spread.half):
@@ -447,9 +480,10 @@
             like((rows, w_gate_full.shape[1]), bf16),
             like((w_down.shape[0], w_down.shape[1] * n), bf16),
         ),
-        in_specs=[vmem] * 6 + [hbm],
+        in_specs=[vmem] * 4 + [hbm] * 3,
         out_specs=(vmem, vmem, hbm),
-        scratch_shapes=[pltpu.VMEM((rows // CHUNKS, features), bf16), pltpu.VMEM((rows, features), bf16)]
+        scratch_shapes=[pltpu.VMEM(w_gate_full.shape, bf16), pltpu.VMEM(w_up_full.shape, bf16), dma((2,))]
+        + [pltpu.VMEM((rows // CHUNKS, features), bf16), pltpu.VMEM((rows, features), bf16)]
         + reduce_scratch(rows, width, n_mp) + gather_sems(DOWN_PIECES, n)
         + [dma((CHUNKS, n_mp // 2)) for _ in range(4)],
         compiler_params=pltpu.CompilerParams(
@@ -498,37 +532,15 @@
     n, n_mp, hidden_in, w_qkv, w_out, attn_gain, mlp_gain, w_gate, w_up, w_down, k_cache, v_cache, cache_len
 ):
     new_count = hidden_in.shape[0]
-    width = w_qkv.shape[2]
-    heads_local = width // HD
     full_rows, w_qkv_full = gather_first(n, n_mp, hidden_in, w_qkv)
-    normed = rms_scale(full_rows, attn_gain)
-    columns = normed
-    projected = jnp.einsum(
-        "nd,kdw->knw",
-        columns,
-        w_qkv_full,
-        preferred_element_type=jnp.float32,
-    )
-    length = cache_len[0]
-    positions = (length + jnp.arange(new_count, dtype=jnp.int32)).astype(jnp.float32)
-    queries = rotate(projected[0].reshape(new_count, heads_local, HD), positions).astype(
-        jnp.bfloat16
-    )
-    fresh_keys = rotate(projected[1].reshape(new_count, heads_local, HD), positions).astype(
-        jnp.bfloat16
-    )
-    fresh_values = projected[2].astype(jnp.bfloat16).reshape(new_count, heads_local, HD)
-    attn, w_out_full, w_gate_full, w_up_full = attend_and_gather(
-        n, cache_len, queries.reshape(new_count, width), fresh_keys.reshape(new_count, width),
-        fresh_values.reshape(new_count, width), k_cache, v_cache, w_out, w_gate, w_up)
+    positions = (cache_len[0] + jnp.arange(new_count, dtype=jnp.int32)).astype(jnp.float32)
+    cosine, sine = rotation(positions)
+    attn, fresh_keys, fresh_values, w_out_full, w_gate_full, w_up_full = attend_and_gather(
+        n, cache_len, full_rows, attn_gain, w_qkv_full, cosine, sine, k_cache, v_cache, w_out, w_gate, w_up)
     mid_local, units, w_down_full = middle(
         n, n_mp, attn, w_out_full, hidden_in, mlp_gain, w_gate_full, w_up_full, w_down)
     hidden_out = last(n_mp, units, w_down_full, mid_local)
-    return (
-        hidden_out,
-        fresh_keys.reshape(new_count, width),
-        fresh_values.reshape(new_count, width),
-    )
+    return hidden_out, fresh_keys, fresh_values
 
 
 def solution(mesh):

time: 556 us -> 496 us (0.89)
  Pallas kernels: 522 us -> 481 us
  matrix products: 9.32 us -> 0 us
  other arithmetic: 7.83 us -> 0.57 us
  local copies, waits for them, and re-layouts: 15.3 us -> 8.8 us
    pallas_call x1, Pallas kernels: 153 us -> 116 us  [middle(): pl.pallas_call(functools.partial(middle_kernel, n, n_mp), out_shape=(like...]
    dot_general x1 -> x0, matrix products: 9.32 us -> none  [on_device(): jnp.einsum('nd,kdw->knw', columns, w_qkv_full, preferred_element_type=jnp...]
    slice x3 -> x0, local copies, waits for them, and re-layouts: 7.31 us -> none  [the longest x2 4.39 us: on_device(): projected[1].reshape(new_count, heads_local, HD)]
where the time goes in v3:
time: 496 us; the launch traced here: 491 us
  Pallas kernels  481 us (97%)
  local copies, waits for them, and re-layouts  8.8 us (2%)
    pallas_call x1, Pallas kernels, attend_and_gather(): pl.pallas_call(functools.partial(attention_kernel, n, n_pairs, n_blocks),...  243 us
    pallas_call x1, Pallas kernels, middle(): pl.pallas_call(functools.partial(middle_kernel, n, n_mp), out_shape=(like...  116 us
    pallas_call x1, Pallas kernels, gather_first(): pl.pallas_call(functools.partial(first_kernel, n, n_mp), out_shape=(jax.S...  86 us
    pallas_call x1, Pallas kernels, last(): pl.pallas_call(functools.partial(last_kernel, n_mp), out_shape=jax.ShapeD...  35.5 us

profile of v3, /device:TPU:0, one launch (start us, length us, event | category | flops | bytes accessed | tf_op | source)
XLA Modules:
  0.0 491.3 jit_solution(3840696360053407741)
XLA Ops:
  1.3 1.3 reshape.57.gain
  2.6 1.3 reshape.58.gain
  3.9 0.5 fusion
  4.5 1.0 copy.15.sine
  5.6 1.0 copy.14.cosine
  6.5 86.0 %shard_map.130 = (bf16[1024,2048]{1,0:T(8,128)(2,1)}, bf16[3,2048,512]{2,1,0:T(8,128)(2,1)}) custom-call(bf16[1024,512]{1,0:T(8,128)(2,1)} %hidden.1, bf16[3,256,512]{2,1,0:T(8,128)(2,1)} %wqkv.1), custom_call_target="tpu_custom_call" | custom-call | tf_op jit(solution)/shard_map/pallas_call | solution.py:137
  92.6 243.0 %shard_map.131 = (bf16[1024,512]{1,0:T(8,128)(2,1)}, bf16[1024,512]{1,0:T(8,128)(2,1)}, bf16[1024,512]{1,0:T(8,128)(2,1)}, bf16[512,2048]{1,0:T(8,128)(2,1)}, bf...) custom-call(s32[1]{0:T(128)} %copy.19.length_ref, bf16[1024,2048]{1,0:T(8,128)(2,1)} %get-tuple-element.14.hidden, ...), custom_call_target="tpu_custom_call" | custom-call | tf_op jit(solution)/shard_map/pallas_call | solution.py:280
  335.6 116.0 %shard_map.132 = (bf16[1024,512]{1,0:T(8,128)(2,1)}, bf16[1024,2048]{1,0:T(8,128)(2,1)}, bf16[2048,2048]{1,0:T(8,128)(2,1)}) custom-call(bf16[1024,512]{1,0:T(8,128)(2,1)} %get-tuple-element.16.attn, bf16[512,2048]{1,0:T(8,128)(2,1)} %get-tuple-element.17.w_out, bf16[1024,512]{1,0:T(8,128)(2,1)} %hidden.1, bf16[1,2048]{1,0:T(2,128)(2,1)} %reshape.58.gain, ...), custom_call_target="tpu_custom_call" | custom-call | tf_op jit(solution)/shard_map/pallas_call | solution.py:476
  451.6 0.0 copy-start
  451.6 1.2 copy-done
  452.8 0.0 copy-start.2
  452.8 35.5 %shard_map.133 = bf16[1024,512]{1,0:T(8,128)(2,1)S(1)} custom-call(bf16[1024,2048]{1,0:T(8,128)(2,1)} %get-tuple-element.20.units, bf16[2048,2048]{1,0:T(8,128)(2,1)} %get-tuple-element.21.w_down, bf16[1024,512]{1,0:T(8,128)(2,1)S(1)} %copy-done), custom_call_target="tpu_custom_call" | custom-call | tf_op jit(solution)/shard_map/pallas_call | solution.py:520
  488.3 0.0 copy-start.1
  488.4 1.0 copy.20
  489.3 0.0 copy-done.2
  489.3 1.0 copy.21
  490.3 0.0 copy-done.1
  490.3 1.0 copy.22
  (5 shorter events, 0.1 us)
Async XLA Ops:
  451.6 1.2 copy-start
  452.8 36.5 %copy-start.2 = (bf16[1024,512]{1,0:T(8,128)(2,1)S(1)}, bf16[1024,512]{1,0:T(8,128)(2,1)}, u32[]{:S(2)}) copy-start(bf16[1024,512]{1,0:T(8,128)(2,1)} %get-tuple-element.32) | copy-start | bytes 3145732
  488.3 2.0 copy-start.1

commit v4 on v3

--- a/solution.py
+++ b/solution.py
@@ -86,9 +86,110 @@
             self.own(c).wait()
 
 
+class Chain:
+    def __init__(self, n, pieces, sems):
+        self.half = n // 2
+        self.pieces = pieces
+        self.send_far, self.recv_far, self.send_near, self.recv_near, self.own_sem = sems
+        self.me = lax.axis_index("req")
+        self.group, self.parity = self.me // 2, lax.rem(self.me, 2)
+        self.partner = self.me + 1 - 2 * self.parity
+        self.ticks = len(pieces) + self.half
+
+    def greet(self, barrier):
+        for shift in range(1, self.half):
+            other = lax.rem(self.group + shift, self.half) * 2 + self.parity
+            pl.semaphore_signal(barrier, inc=1, device_id={"req": other}, device_id_type=MESH)
+        pl.semaphore_signal(barrier, inc=1, device_id={"req": self.partner}, device_id_type=MESH)
+        return self.half
+
+    def shards(self, c):
+        return (0, 1) if c == 0 else (0,)
+
+    def within(self, group):
+        return (group >= 0) & (group < self.half)
+
+    def owner(self, way, hop, b):
+        side = self.parity if b == 0 else 1 - self.parity
+        return (self.group - way * hop) * 2 + side
+
+    def far(self, c, way, hop, b, arriving=False):
+        src, slot = self.pieces[c]
+        place = slot(self.owner(way, hop if arriving else hop - 1, b))
+        index = ((way + 1) // 2 * self.half + hop) * 2 + b
+        return pltpu.make_async_remote_copy(
+            src_ref=src if hop == 1 and b == 0 and not arriving else place, dst_ref=place,
+            send_sem=self.send_far.at[c, index], recv_sem=self.recv_far.at[c, index],
+            device_id={"req": (self.group + way) * 2 + self.parity}, device_id_type=MESH)
+
+    def near(self, c, way, hop):
+        src, slot = self.pieces[c]
+        place = slot(self.owner(way, hop, 0))
+        index = (way + 1) // 2 * self.half + hop
+        return pltpu.make_async_remote_copy(
+            src_ref=src if hop == 0 else place, dst_ref=place, send_sem=self.send_near.at[c, index],
+            recv_sem=self.recv_near.at[c, index], device_id={"req": self.partner}, device_id_type=MESH)
+
+    def own(self, c):
+        src, slot = self.pieces[c]
+        return pltpu.make_async_copy(src, slot(self.me), self.own_sem.at[c])
+
+    def send(self, c, hop):
+        for way in (-1, 1):
+            @pl.when(self.within(self.group + way) & self.within(self.group - way * (hop - 1)))
+            def _(way=way):
+                for b in self.shards(c):
+                    self.far(c, way, hop, b).start()
+
+    def start(self):
+        for c in range(len(self.pieces)):
+            self.near(c, 1, 0).start()
+            self.own(c).start()
+            if c > 0:
+                self.send(c, 1)
+
+    def relay(self, c, hop):
+        for way in (-1, 1):
+            @pl.when(self.within(self.group - way * hop))
+            def _(way=way):
+                for b in self.shards(c):
+                    self.far(c, way, hop, b, arriving=True).wait_recv()
+                if c > 0:
+                    self.near(c, way, hop).start()
+        if hop < self.half - 1:
+            self.send(c, hop + 1)
+
+    def tick(self, t):
+        for c in range(len(self.pieces)):
+            hop = t - c + (c > 0)
+            if c == 0 and hop == 0:
+                self.near(0, 1, 0).wait_recv()
+                self.send(0, 1)
+            elif 1 <= hop < self.half:
+                self.relay(c, hop)
+
+    def finish(self):
+        for c in range(len(self.pieces)):
+            self.near(c, 1, 0).wait_send()
+            if c > 0:
+                self.near(c, 1, 0).wait_recv()
+            self.own(c).wait()
+            for hop in range(1, self.half):
+                for way in (-1, 1):
+                    @pl.when(self.within(self.group + way) & self.within(self.group - way * (hop - 1)))
+                    def _(way=way, hop=hop, c=c):
+                        for b in self.shards(c):
+                            self.far(c, way, hop, b).wait_send()
+
+                    if c > 0:
+                        @pl.when(self.within(self.group - way * hop))
+                        def _(way=way, hop=hop, c=c):
+                            self.near(c, way, hop).wait()
+
+
 def gather_sems(pieces, n):
     dma = pltpu.SemaphoreType.DMA
-    return [dma((pieces, n // 2)) for _ in range(4)] + [dma((pieces,))]
+    return [dma((pieces, 2 * n)) for _ in range(2)] + [dma((pieces, n)) for _ in range(2)] + [dma((pieces,))]
 
 
 def first_kernel(n, n_mp, hid, wqkv, hid_full, wqkv_full, *sems):
@@ -101,7 +202,7 @@
              i, pl.ds(pl.multiple_of(r * depth + part * rows, rows), rows)])
         for i in range(3) for part in range(2)
     ]
-    gather = Gather("req", n, pieces, sems[:5])
+    gather = Chain(n, pieces, sems[:5])
     me = lax.axis_index("mp")
     barrier = pltpu.get_barrier_semaphore()
     expected = gather.greet(barrier)
@@ -116,15 +217,13 @@
         for shift in range(1, n_mp)
     ]
     own = pltpu.make_async_copy(hid, mine, mp_own)
-    for c in range(6):
-        gather.start(c)
     for copy in copies:
         copy.start()
     own.start()
-    for c in range(6):
-        gather.forward(c)
-    for c in range(6):
-        gather.finish(c)
+    gather.start()
+    for t in range(gather.ticks):
+        gather.tick(t)
+    gather.finish()
     for copy in copies:
         copy.wait()
     own.wait()
@@ -237,14 +336,13 @@
                 src.at[pl.ds(part * rows, rows)],
                 lambda r, full=full, part=part, depth=depth, rows=rows: full.at[
                     pl.ds(pl.multiple_of(r * depth + part * rows, rows), rows)]))
-    gather = Gather("req", n, pieces, sems)
+    gather = Chain(n, pieces, sems)
 
     @pl.when(step == 0)
     def _():
         barrier = pltpu.get_barrier_semaphore()
         pl.semaphore_wait(barrier, gather.greet(barrier))
-        for c in range(PIECES):
-            gather.start(c)
+        gather.start()
         project(hidden, gain, w_qkv, cosine, sine, queries, keys, values)
 
     rows = out_ref.shape[0]
@@ -252,15 +350,14 @@
         length_ref[0], pl.program_id(0), pl.program_id(1) * rows, rows, queries, keys, values, kc_ref, vc_ref,
         out_ref)
 
-    for c in range(PIECES):
-        @pl.when(step == min(c, steps - 1))
-        def _(c=c):
-            gather.forward(c)
+    for t in range(gather.ticks):
+        @pl.when(step == min(t, steps - 1))
+        def _(t=t):
+            gather.tick(t)
 
     @pl.when(step == steps - 1)
     def _():
-        for c in range(PIECES):
-            gather.finish(c)
+        gather.finish()
 
 
 def attend_and_gather(n, length, hidden, gain, w_qkv, cosine, sine, k_cache, v_cache, w_out, w_gate, w_up):
@@ -401,14 +498,13 @@
     def mid_block(c, r):
         return mid_full.at[pl.ds(c * step, step), pl.ds(pl.multiple_of(r * width, width), width)]
 
-    down = Gather("req", n, pieces, sems[4:9])
+    down = Chain(n, pieces, sems[4:9])
     spread = Gather(
         "mp", n_mp, [(mid_block(c, me), lambda r, c=c: mid_block(c, r)) for c in range(CHUNKS)],
         sems[9:13] + (None,))
     barrier = pltpu.get_barrier_semaphore()
     pl.semaphore_wait(barrier, down.greet(barrier) + spread.greet(barrier))
-    for p in range(DOWN_PIECES):
-        down.start(p)
+    down.start()
     loads = [
         pltpu.make_async_copy(w_gate_full, gate_in, load_sems.at[0]),
         pltpu.make_async_copy(w_up_full, up_in, load_sems.at[1]),
@@ -435,8 +531,8 @@
             mid_chunk(c - 2)
         if 3 <= c:
             spread.forward(c - 3)
-        if 2 <= c:
-            down.forward(c - 2)
+        if 1 <= c:
+            down.tick(c - 1)
     for load in loads:
         load.wait()
     columns = units.shape[1]
@@ -455,16 +551,16 @@
             upper = jnp.dot(normed[...], up_in[:, cols], preferred_element_type=jnp.float32)
             units[chunk_rows(c), cols] = (gate * jax.nn.sigmoid(gate) * upper).astype(units.dtype)
 
-        if CHUNKS + 1 + c < DOWN_PIECES:
-            down.forward(CHUNKS + 1 + c)
+        down.tick(CHUNKS + 2 + c)
+    for t in range(2 * CHUNKS + 2, down.ticks):
+        down.tick(t)
     for c in range(CHUNKS):
         reduce.finish(c)
         for shift in range(1, spread.half):
             spread.far(c, shift).wait_send()
         for shift in range(spread.half):
             spread.near(c, shift).wait_send()
-    for p in range(DOWN_PIECES):
-        down.finish(p)
+    down.finish()
 
 
 def middle(n, n_mp, attn, w_out_full, hidden_in, gain, w_gate_full, w_up_full, w_down):

time: 496 us -> 459 us (0.925)
  Pallas kernels: 481 us -> 448 us
    pallas_call x1, Pallas kernels: 243 us -> 223 us  [attend_and_gather(): pl.pallas_call(functools.partial(attention_kernel, n, n_pairs, n_blocks),...]
    pallas_call x1, Pallas kernels: 116 us -> 106 us  [middle(): pl.pallas_call(functools.partial(middle_kernel, n, n_mp), out_shape=(like...]
where the time goes in v4:
time: 459 us
  Pallas kernels  448 us (98%)
  local copies, waits for them, and re-layouts  8.8 us (2%)
    pallas_call x1, Pallas kernels, attend_and_gather(): pl.pallas_call(functools.partial(attention_kernel, n, n_pairs, n_blocks),...  223 us
    pallas_call x1, Pallas kernels, middle(): pl.pallas_call(functools.partial(middle_kernel, n, n_mp), out_shape=(like...  106 us
    pallas_call x1, Pallas kernels, gather_first(): pl.pallas_call(functools.partial(first_kernel, n, n_mp), out_shape=(jax.S...  83.5 us
    pallas_call x1, Pallas kernels, last(): pl.pallas_call(functools.partial(last_kernel, n_mp), out_shape=jax.ShapeD...  35.3 us

profile of v4, /device:TPU:0, one launch (start us, length us, event | category | flops | bytes accessed | tf_op | source)
XLA Modules:
  0.0 459.2 jit_solution(13239425363084066838)
XLA Ops:
  1.3 1.3 reshape.57.gain
  2.6 1.3 reshape.58.gain
  3.9 0.5 fusion
  4.5 1.0 copy.15.sine
  5.6 1.0 copy.14.cosine
  6.5 83.5 %shard_map.130 = (bf16[1024,2048]{1,0:T(8,128)(2,1)}, bf16[3,2048,512]{2,1,0:T(8,128)(2,1)}) custom-call(bf16[1024,512]{1,0:T(8,128)(2,1)} %hidden.1, bf16[3,256,512]{2,1,0:T(8,128)(2,1)} %wqkv.1), custom_call_target="tpu_custom_call" | custom-call | tf_op jit(solution)/shard_map/pallas_call | solution.py:236
  90.0 223.4 %shard_map.131 = (bf16[1024,512]{1,0:T(8,128)(2,1)}, bf16[1024,512]{1,0:T(8,128)(2,1)}, bf16[1024,512]{1,0:T(8,128)(2,1)}, bf16[512,2048]{1,0:T(8,128)(2,1)}, bf...) custom-call(s32[1]{0:T(128)} %copy.19.length_ref, bf16[1024,2048]{1,0:T(8,128)(2,1)} %get-tuple-element.14.hidden, ...), custom_call_target="tpu_custom_call" | custom-call | tf_op jit(solution)/shard_map/pallas_call | solution.py:377
  313.4 106.3 %shard_map.132 = (bf16[1024,512]{1,0:T(8,128)(2,1)}, bf16[1024,2048]{1,0:T(8,128)(2,1)}, bf16[2048,2048]{1,0:T(8,128)(2,1)}) custom-call(bf16[1024,512]{1,0:T(8,128)(2,1)} %get-tuple-element.16.attn, bf16[512,2048]{1,0:T(8,128)(2,1)} %get-tuple-element.17.w_out, bf16[1024,512]{1,0:T(8,128)(2,1)} %hidden.1, bf16[1,2048]{1,0:T(2,128)(2,1)} %reshape.58.gain, ...), custom_call_target="tpu_custom_call" | custom-call | tf_op jit(solution)/shard_map/pallas_call | solution.py:572
  419.7 0.0 copy-start
  419.7 1.2 copy-done
  421.0 0.0 copy-start.2
  421.0 35.3 %shard_map.133 = bf16[1024,512]{1,0:T(8,128)(2,1)S(1)} custom-call(bf16[1024,2048]{1,0:T(8,128)(2,1)} %get-tuple-element.20.units, bf16[2048,2048]{1,0:T(8,128)(2,1)} %get-tuple-element.21.w_down, bf16[1024,512]{1,0:T(8,128)(2,1)S(1)} %copy-done), custom_call_target="tpu_custom_call" | custom-call | tf_op jit(solution)/shard_map/pallas_call | solution.py:616
  456.3 0.0 copy-start.1
  456.3 1.0 copy.20
  457.3 0.0 copy-done.2
  457.3 1.0 copy.21
  458.2 0.0 copy-done.1
  458.2 1.0 copy.22
  (5 shorter events, 0.1 us)
Async XLA Ops:
  419.7 1.2 copy-start
  421.0 36.3 %copy-start.2 = (bf16[1024,512]{1,0:T(8,128)(2,1)S(1)}, bf16[1024,512]{1,0:T(8,128)(2,1)}, u32[]{:S(2)}) copy-start(bf16[1024,512]{1,0:T(8,128)(2,1)} %get-tuple-element.32) | copy-start | bytes 3145732
  456.3 2.0 copy-start.1
